TPU v7x, 32 devices: a whole 2x2x4 slice. The times are simulated.
32 devices in a mesh: grp: 2 (over y), head: 4 (over z), tm: 4 (over x, core).
Axes of the slice: x: 2, y: 2, z: 4, core: 2. Of those that a mesh axis runs over, the one named last changes fastest.
Arguments:
- query_rows: bfloat16 [32, 64, 3072], P(('grp', 'tm'), 'head'), parts along dimension 0, may hold values from -180 to 180
- key_rows: bfloat16 [32, 64, 3072], P(('grp', 'tm'), 'head'), parts along dimension 0, may hold values from -6 to 6
- value_rows: bfloat16 [32, 64, 3072], P(('grp', 'tm'), 'head'), parts along dimension 0, may hold values from -6 to 6
- pair_list: int32 [32, 32], P('grp'), parts along dimension 0, may hold values from 0 to 15, as said below
- block_tokens: int32 [32], P('grp'), parts along dimension 0, may hold values from 1 to 64, 768 in all
Outputs:
- attended: bfloat16 [32, 64, 3072], P(('grp', 'tm'), 'head'), parts along dimension 0
There are 2 independent parts, one for each index of `grp`. A program takes and returns all parts, laid end to end along the dimension named above; each array names one. Nothing has to cross between parts.
Inputs may be any that keep to these rules, and one draw needn't show every extreme that they name: `pair_list`: row q names q in column 0 and q xor 1 in column 1; a block may be named twice in a row. The query blocks of one time shard name at most 2 different blocks of a time shard beside it and at most 1 of a time shard two or more away; both bounds are reached.
All inputs are finite; a program needn't handle non-finite values.
Results may differ from a plain program's by a relative error of at most 0.0012.
The roundings to bfloat16 on the way count: a program that leaves them out, or rounds other values in their place, can miss the bound.
Values may be sent and summed in bfloat16 or wider, within the bound.
No kernel may reach another device: no remote copies, remote signals or barrier semaphores. Data moves between devices by JAX's collectives and lax.ppermute only.
A program may use at most 128 MiB of HBM per device.

v0:
```python
import functools
import math

import jax
import jax.numpy as jnp
from jax import lax
from jax.experimental import pallas as pl
from jax.experimental.pallas import tpu as pltpu
from jax.sharding import PartitionSpec as P

HD = 128
BLK = 64
NEAR_CAP = 2
FAR_CAP = 1
NEG = -1e30
ROTATE_SCALE = 1.0 / math.sqrt(HD)
SCORE_SCALE = 1.0 / math.sqrt(HD)
VMEM = 24 * 1024 * 1024
WIDE_VMEM = 60 * 1024 * 1024
TOKEN = jax.ShapeDtypeStruct((8, 128), jnp.float32)
NO_COST = pl.CostEstimate(flops=0, bytes_accessed=0, transcendentals=0)
HIGH_COST = pl.CostEstimate(flops=10**11, bytes_accessed=0, transcendentals=0)
LOG2E = math.log2(math.e)


def sign_matrix():
    common = lax.broadcasted_iota(jnp.int32, (HD, HD), 0) & lax.broadcasted_iota(
        jnp.int32, (HD, HD), 1
    )
    bits = HD.bit_length() - 1
    parity = common
    for bit in range(1, bits):
        parity = parity ^ (common >> bit)
    return jnp.where((parity & 1) == 0, 1.0, -1.0).astype(jnp.bfloat16)


def rows_of(block):
    rows, width = math.prod(block.shape[:-1]), block.shape[-1]
    if block.shape[-2] % 16 == 0:
        return block.reshape(rows, width)
    return block.astype(jnp.float32).reshape(rows, width).astype(block.dtype)


def by_distance(refs, count, direction, axis="head"):
    if len(refs) > 1:
        return list(refs)
    me = lax.axis_index(axis)
    return [refs[0].at[lax.rem(me + direction * s + count, count)] for s in range(count)]


def rotate_kernel(group, count_head, skipped, *refs):
    ids, start, size = group
    count = len(ids)
    sources, outs = refs[:count], by_distance(refs[count + skipped : -3], count_head, 1)
    token, buffer, sems = refs[-3:]
    token[...] = jnp.zeros_like(token)
    blocks, tokens, width = sources[0].shape
    width_here = width // count_head
    me = lax.axis_index("head")
    order = list(range(1, count_head)) + [0]
    copies = {}
    for s in order:
        goal = lax.rem(me + s, count_head)
        column = pl.multiple_of(goal * width_here + start, HD)
        for k, source in enumerate(sources):
            copies[s, k] = pltpu.make_async_copy(
                source.at[:, :, pl.ds(column, size)], buffer.at[s, k], sems.at[s, k]
            )
            copies[s, k].start()
    sign = sign_matrix()
    for s in order:
        for k in range(count):
            copies[s, k].wait()
            flat = rows_of(buffer[s, k])
            heads = [flat[:, at : at + HD] for at in range(0, size, HD)]
            turned = jnp.dot(
                jnp.concatenate(heads, axis=0), sign, preferred_element_type=jnp.float32
            )
            turned = (turned * ROTATE_SCALE).reshape(size // HD, blocks, tokens, HD)
            for h in range(size // HD):
                outs[s][k, :, :, h * HD : (h + 1) * HD] = turned[h].astype(jnp.bfloat16)


def rotate_pieces(sources, start, size, count_head, stacked, after=(), limit=VMEM):
    blocks, tokens, _ = sources[0].shape
    count = len(sources)
    one = (count, blocks, tokens, size)
    shapes = [(count_head,) + one] if stacked else [one] * count_head
    *pieces, token = pl.pallas_call(
        functools.partial(
            rotate_kernel, (tuple(range(count)), start, size), count_head, len(after)
        ),
        in_specs=[pl.BlockSpec(memory_space=pltpu.HBM)] * count
        + [pl.BlockSpec(memory_space=pl.ANY)] * len(after),
        out_specs=[pl.BlockSpec(memory_space=pltpu.VMEM)] * (len(shapes) + 1),
        out_shape=[jax.ShapeDtypeStruct(shape, jnp.bfloat16) for shape in shapes] + [TOKEN],
        scratch_shapes=[
            pltpu.VMEM((count_head,) + one, jnp.bfloat16),
            pltpu.SemaphoreType.DMA((count_head, count)),
        ],
        cost_estimate=NO_COST,
        compiler_params=pltpu.CompilerParams(vmem_limit_bytes=limit),
    )(*sources, *after)
    return pieces, token


def slots_at(distance, count_tm):
    return NEAR_CAP if distance in (1, count_tm - 1) else FAR_CAP


def pick_kernel(count_head, count_tm, own_count, skipped, picks_ref, *refs):
    pieces = by_distance(refs[:own_count], count_head, -1)
    outs = by_distance(refs[own_count + skipped :], count_tm, 1, "tm")[-(count_tm - 1) :]
    shard = lax.axis_index("tm")
    for distance, out in enumerate(outs, 1):
        goal = lax.rem(shard + distance, count_tm)
        for k in range(slots_at(distance, count_tm)):
            pick = picks_ref[NEAR_CAP * goal + k]
            for s in range(count_head):
                out[k, s] = pieces[s][:, pick]


def pick_blocks(picks, owns, count_head, count_tm, stacked, after=(), cost=NO_COST):
    kinds, _, tokens, width = owns[0].shape[-4:]
    one = (count_head, kinds, tokens, width)
    if stacked:
        shapes = [(count_tm, NEAR_CAP) + one]
    else:
        shapes = [(slots_at(distance, count_tm),) + one for distance in range(1, count_tm)]
    vmem = pl.BlockSpec(memory_space=pltpu.VMEM)
    return pl.pallas_call(
        functools.partial(pick_kernel, count_head, count_tm, len(owns), len(after)),
        in_specs=[pl.BlockSpec(memory_space=pltpu.SMEM)]
        + [vmem] * len(owns)
        + [pl.BlockSpec(memory_space=pl.ANY)] * len(after),
        out_specs=[vmem] * len(shapes),
        out_shape=[jax.ShapeDtypeStruct(shape, jnp.bfloat16) for shape in shapes],
        cost_estimate=cost,
        compiler_params=pltpu.CompilerParams(vmem_limit_bytes=VMEM),
    )(picks, *owns, *after)


def remote_rows(count_tm):
    return [
        (distance, k)
        for distance in range(1, count_tm)
        for k in range(slots_at(distance, count_tm))
    ]


def split(value, by):
    if by & (by - 1) == 0:
        return value >> (by.bit_length() - 1), value & (by - 1)
    return lax.div(value, by), lax.rem(value, by)


def plan_kernel(count_head, count_tm, blocks, pair_ref, tokens_ref, _, picks_ref, bias_ref, named_ref, table_ref, sem):
    total_blocks, columns = pair_ref.shape
    pairs = pair_ref[...]
    lane = lax.broadcasted_iota(jnp.int32, named_ref.shape, 1)
    named = jnp.zeros(named_ref.shape, jnp.int32)
    for c in range(columns):
        named = jnp.where(pairs[:, c : c + 1] == lane, 1, named)
    named_ref[...] = named
    copy = pltpu.make_async_copy(named_ref, table_ref, sem)
    copy.start()
    copy.wait()
    shard = lax.axis_index("tm")
    place = lax.axis_index("head")
    mine = shard * blocks

    def two_picks(wanted):
        picks = [jnp.int32(0)] * NEAR_CAP
        count = jnp.int32(0)
        for j in range(blocks):
            for k in range(NEAR_CAP):
                picks[k] = jnp.where((wanted[j] > 0) & (count == k), j, picks[k])
            count = count + wanted[j]
        return picks, count

    def named_by(rows, column):
        found = table_ref[rows, column]
        for i in range(1, blocks):
            found = found | table_ref[rows + i, column]
        return found

    for d in range(count_tm):
        picks, _ = two_picks([named_by(d * blocks, mine + j) for j in range(blocks)])
        for k in range(NEAR_CAP):
            picks_ref[NEAR_CAP * d + k] = picks[k]

    kept = [[table_ref[mine + i, mine + j] * tokens_ref[mine + j] for j in range(blocks)] for i in range(blocks)]
    arrivals = {}
    for distance, k in remote_rows(count_tm):
        first = lax.rem(shard - distance + count_tm, count_tm) * blocks
        if k == 0:
            arrivals[distance] = two_picks([named_by(mine, first + j) for j in range(blocks)])
        picks, count = arrivals[distance]
        there = first + picks[k]
        live = jnp.where(count > k, tokens_ref[there], 0)
        for i in range(blocks):
            kept[i].append(table_ref[mine + i, there] * live)

    total = bias_ref.shape[1]
    piece_rows = BLK // count_head
    at = lax.broadcasted_iota(jnp.int32, (blocks, total), 1)
    query = lax.broadcasted_iota(jnp.int32, (blocks, total), 0)
    own = at < blocks * BLK
    group, token = split(at, piece_rows)
    own_piece, own_block = split(group, blocks)
    far_row, far_group = split(group, count_head)
    row = jnp.where(own, own_block, far_row)
    piece = jnp.where(own, own_piece, far_group)
    source = jnp.where(piece > place, place - piece + count_head, place - piece)
    position = source * piece_rows + token
    limit = jnp.zeros((blocks, total), jnp.int32)
    for r in range(len(kept[0])):
        value = jnp.zeros((blocks, total), jnp.int32)
        for i in range(blocks):
            value = jnp.where(query == i, kept[i][r], value)
        limit = jnp.where(row == r, value, limit)
    bias_ref[...] = jnp.where(position < limit, 0.0, NEG)


def plan(pair_list, block_tokens, after, blocks, count_head, count_tm):
    total_blocks = pair_list.shape[0]
    lanes = -(-total_blocks // 128) * 128
    total = (blocks + len(remote_rows(count_tm))) * BLK
    return pl.pallas_call(
        functools.partial(plan_kernel, count_head, count_tm, blocks),
        in_specs=[
            pl.BlockSpec(memory_space=pltpu.VMEM),
            pl.BlockSpec(memory_space=pltpu.SMEM),
            pl.BlockSpec(memory_space=pl.ANY),
        ],
        out_specs=[pl.BlockSpec(memory_space=pltpu.SMEM), pl.BlockSpec(memory_space=pltpu.VMEM)],
        out_shape=[
            jax.ShapeDtypeStruct((NEAR_CAP * count_tm,), jnp.int32),
            jax.ShapeDtypeStruct((blocks, total), jnp.float32),
        ],
        scratch_shapes=[
            pltpu.VMEM((total_blocks, lanes), jnp.int32),
            pltpu.SMEM((total_blocks, lanes), jnp.int32),
            pltpu.SemaphoreType.DMA,
        ],
        cost_estimate=NO_COST,
        compiler_params=pltpu.CompilerParams(vmem_limit_bytes=VMEM),
    )(pair_list, block_tokens, after)


def attend_kernel(counts, start, tokens_ref, bias_ref, *refs):
    count_head, count_tm, query_count, own_count, slot_count, skipped = counts
    at = [query_count, query_count + own_count, query_count + own_count + slot_count]
    queries = by_distance(refs[: at[0]], count_head, -1)
    owns = by_distance(refs[at[0] : at[1]], count_head, -1)
    slots = by_distance(refs[at[1] : at[2]], count_tm, -1, "tm")[-(count_tm - 1) :]
    outs = by_distance(refs[at[2] + skipped :], count_head, -1)
    _, blocks, tokens, size = owns[0].shape
    shard = lax.axis_index("tm")
    me = lax.axis_index("head")
    sign = sign_matrix()
    for h in range(size // HD):
        lanes = slice(h * HD, (h + 1) * HD)
        query_lanes = slice(start + h * HD, start + (h + 1) * HD)
        query = jnp.concatenate(
            [rows_of(queries[s][0, i, :, query_lanes]) for i in range(blocks) for s in range(count_head)],
            axis=0,
        )

        def gathered(kind):
            pieces = [rows_of(own[kind, :, :, lanes]) for own in owns]
            pieces += [
                rows_of(slots[distance - 1][k, :, kind, :, lanes])
                for distance, k in remote_rows(count_tm)
            ]
            return jnp.concatenate(pieces, axis=0)

        keys, values = gathered(0), gathered(1)
        total = keys.shape[0]
        dots = lax.dot_general(
            query, keys, (((1,), (1,)), ((), ())), preferred_element_type=jnp.float32
        )
        dots = dots.reshape(blocks, BLK, total) + bias_ref[...][:, None, :]
        peak = jnp.max(dots, axis=-1, keepdims=True)
        weights = jnp.exp2((dots - peak) * (SCORE_SCALE * LOG2E))
        denominator = jnp.sum(weights, axis=-1, keepdims=True).reshape(blocks * BLK, 1)
        weights_half = weights.astype(jnp.bfloat16).reshape(blocks * BLK, total)
        mixed = jnp.dot(weights_half, values, preferred_element_type=jnp.float32) / denominator
        turned = jnp.zeros_like(mixed)
        rest = mixed
        for _ in range(3):
            piece = rest.astype(jnp.bfloat16)
            turned = turned + jnp.dot(piece, sign, preferred_element_type=jnp.float32)
            rest = rest - piece.astype(jnp.float32)
        turned = (turned * ROTATE_SCALE).reshape(blocks, count_head, tokens, HD)
        token = lax.broadcasted_iota(jnp.int32, (tokens, HD), 0)
        for s in range(count_head):
            position = lax.rem(me - s + count_head, count_head) * tokens + token
            for i in range(blocks):
                outs[s][i, :, lanes] = jnp.where(
                    position < tokens_ref[shard * blocks + i], turned[i, s], 0.0
                ).astype(jnp.bfloat16)


def attend(block_tokens, bias, start, queries, owns, slots, count_head, count_tm, after, cost):
    _, blocks, tokens, size = owns[0].shape[-4:]
    shapes = [(blocks, tokens, size)] * count_head
    counts = (count_head, count_tm, len(queries), len(owns), len(slots), len(after))
    vmem = pl.BlockSpec(memory_space=pltpu.VMEM)
    return pl.pallas_call(
        functools.partial(attend_kernel, counts, start),
        in_specs=[pl.BlockSpec(memory_space=pltpu.SMEM)]
        + [vmem] * (1 + len(queries) + len(owns) + len(slots))
        + [pl.BlockSpec(memory_space=pl.ANY)] * len(after),
        out_specs=[vmem] * len(shapes),
        out_shape=[jax.ShapeDtypeStruct(shape, jnp.bfloat16) for shape in shapes],
        cost_estimate=cost,
        compiler_params=pltpu.CompilerParams(vmem_limit_bytes=VMEM),
    )(block_tokens, bias, *queries, *owns, *slots, *after)


def place_kernel(counts, starts, width_here, *refs):
    count_head = counts[0]
    out_ref, sems = refs[-2:]
    copies = []
    at = 0
    for count, start in zip(counts[1:], starts):
        pieces = by_distance(refs[at : at + count], count_head, 1)
        at += count
        for s, piece in enumerate(pieces):
            column = lax.rem(lax.axis_index("head") + s, count_head) * width_here + start
            copies.append(
                pltpu.make_async_copy(
                    piece,
                    out_ref.at[:, :, pl.ds(pl.multiple_of(column, HD), piece.shape[-1])],
                    sems.at[len(copies)],
                )
            )
            copies[-1].start()
    for copy in copies:
        copy.wait()


def place_pieces(parts, starts, count_head, width_here):
    pieces = [piece for part in parts for piece in part]
    blocks, tokens, _ = pieces[0].shape[-3:]
    counts = (count_head,) + tuple(len(part) for part in parts)
    return pl.pallas_call(
        functools.partial(place_kernel, counts, starts, width_here),
        in_specs=[pl.BlockSpec(memory_space=pl.ANY)] * len(pieces),
        out_specs=pl.BlockSpec(memory_space=pltpu.HBM),
        out_shape=jax.ShapeDtypeStruct((blocks, tokens, count_head * width_here), jnp.bfloat16),
        scratch_shapes=[pltpu.SemaphoreType.DMA((len(parts) * count_head,))],
        compiler_params=pltpu.CompilerParams(vmem_limit_bytes=VMEM),
    )(*pieces)


def shifted(array, axis, distance):
    count = lax.axis_size(axis)
    return lax.ppermute(array, axis, [(i, (i + distance) % count) for i in range(count)])


def exchange(pieces, direction):
    if len(pieces) == 1:
        return [lax.all_to_all(pieces[0], "head", split_axis=0, concat_axis=0, tiled=True)]
    return [pieces[0]] + [
        shifted(piece, "head", direction * s) for s, piece in enumerate(pieces[1:], 1)
    ]


def forward(sent):
    if len(sent) == 1:
        return [lax.all_to_all(sent[0], "tm", split_axis=0, concat_axis=0, tiled=True)]
    return [shifted(block, "tm", distance) for distance, block in enumerate(sent, 1)]


def shards(query_rows, key_rows, value_rows, pair_list, block_tokens):
    count_head = lax.axis_size("head")
    count_tm = lax.axis_size("tm")
    blocks, tokens, width = query_rows.shape
    width_here = width // count_head
    heads = width_here // HD
    cut = (heads + 1) // 2 * HD
    parts = [(0, cut), (cut, width_here - cut)] if heads > 1 else [(0, width_here)]
    sources = [key_rows, value_rows]
    pieces, token = rotate_pieces(sources, *parts[0], count_head, False, limit=WIDE_VMEM)
    packed = [pieces]
    picks, bias = plan(pair_list, block_tokens, token, blocks, count_head, count_tm)
    for part in parts[1:]:
        pieces, token = rotate_pieces(sources, *part, count_head, False, after=(bias, token))
        packed.append(pieces)
    key_values = [exchange(pieces, 1) for pieces in packed]
    sent = [pick_blocks(picks, key_values[0], count_head, count_tm, False)]
    for owns in key_values[1:]:
        sent.append(
            pick_blocks(
                picks, owns, count_head, count_tm, False, after=(sent[-1][0],), cost=HIGH_COST
            )
        )
    query, _ = rotate_pieces([query_rows], 0, width_here, count_head, False, after=(sent[0][0],))
    queries = exchange(query, 1)
    returned, after = [], ()
    for at, (owns, picked) in enumerate(zip(key_values, sent)):
        cost = NO_COST if at == len(parts) - 1 else HIGH_COST
        slots, start = forward(picked), parts[at][0]
        attended = attend(
            block_tokens, bias, start, queries, owns, slots, count_head, count_tm, after, cost
        )
        after = (attended[0],)
        returned.append(exchange(attended, -1))
    return place_pieces(returned, [start for start, _ in parts], count_head, width_here)


def solution(mesh):
    placed = (
        P(("grp", "tm"), "head", None),
        P(("grp", "tm"), "head", None),
        P(("grp", "tm"), "head", None),
        P("grp", None),
        P("grp"),
    )
    return jax.shard_map(
        shards,
        mesh=mesh,
        in_specs=placed,
        out_specs=P(("grp", "tm"), "head", None),
        check_vma=False,
    )
```

profile of v0, /device:TPU:0, one launch (start us, length us, event | category | flops | bytes accessed | tf_op | source)
XLA Modules:
  0.0 57.0 jit_solution(15365588791161376129)
XLA Ops:
  0.0 0.0 copy-start
  0.0 0.0 copy-start.1
  0.0 2.9 %shard_map.55 = (bf16[2,4,16,384]{3,2,1,0:T(8,128)(2,1)}, bf16[2,4,16,384]{3,2,1,0:T(8,128)(2,1)}, bf16[2,4,16,384]{3,2,1,0:T(8,128)(2,1)}, bf16[2,4,16,384]{3,2,1,0:T(8,128)(2,1)}, f32[8,128]{1,0:T(8,128)}) custom-call(bf16[4,16,3072]{2,1,0:T(8,128)(2,1)} %refs_0_.5, bf16[4,16,3072]{2,1,0:T(8,128)(2,1)} %refs_1_.3), custom_call_target="tpu_custom_call" | custom-call | tf_op jit(solution)/shard_map/pallas_call | solution.py:89
  2.9 0.0 copy-start.4
  2.9 3.1 %collective-permute-start = (bf16[2,4,16,384]{3,2,1,0:T(8,128)(2,1)}, bf16[2,4,16,384]{3,2,1,0:T(8,128)(2,1)S(1)}, u32[]{:S(2)}, u32[]{:S(2)}) collective-permute-start(bf16[2,4,16,384]{3,2,1,0:T(8,128)(2,1)} %get-tuple-element.38), channel_id=1, source_target_pairs={{0,4},{4,8},{8,12},{12,0},{1,5},{5,9},{9,13},{13,1},{2,6},{6,10},{... | collective-permute-start | bytes 294920 | tf_op jit(solution)/shard_map/ppermute | solution.py:360
  6.0 2.6 %collective-permute-start.1 = (bf16[2,4,16,384]{3,2,1,0:T(8,128)(2,1)}, bf16[2,4,16,384]{3,2,1,0:T(8,128)(2,1)S(1)}, u32[]{:S(2)}, u32[]{:S(2)}) collective-permute-start(bf16[2,4,16,384]{3,2,1,0:T(8,128)(2,1)} %get-tuple-element.39), channel_id=1, source_target_pairs={{0,8},{4,12},{8,0},{12,4},{1,9},{5,13},{9,1},{13,5},{2,10},{6,14},... | collective-permute-start | bytes 294920 | tf_op jit(solution)/shard_map/ppermute | solution.py:360
  8.5 0.0 copy-start.6
  8.6 1.3 %collective-permute-start.2 = (bf16[2,4,16,384]{3,2,1,0:T(8,128)(2,1)}, bf16[2,4,16,384]{3,2,1,0:T(8,128)(2,1)S(1)}, u32[]{:S(2)}, u32[]{:S(2)}) collective-permute-start(bf16[2,4,16,384]{3,2,1,0:T(8,128)(2,1)} %get-tuple-element.40), channel_id=1, source_target_pairs={{0,12},{4,0},{8,4},{12,8},{1,13},{5,1},{9,5},{13,9},{2,14},{6,2},{... | collective-permute-start | bytes 294920 | tf_op jit(solution)/shard_map/ppermute | solution.py:360
  9.9 0.0 copy-done.4
  9.9 0.0 copy-done.6
  9.9 0.7 %copy-done.5 = s32[16,32]{1,0:T(8,128)S(1)} copy-done((s32[16,32]{1,0:T(8,128)S(1)}, s32[16,32]{1,0:T(8,128)}, u32[]{:S(2)}) %copy-start.5) | copy-done | bytes 2072
  10.6 2.3 %shard_map.56 = (s32[8]{0:T(128)S(1)}, f32[4,576]{1,0:T(4,128)S(1)}) custom-call(s32[16,32]{1,0:T(8,128)S(1)} %copy-done.5, s32[16]{0:T(128)S(1)} %copy-done.6, f32[8,128]{1,0:T(8,128)S(1)} %copy-done.4), custom_call_target="tpu_custom_call" | custom-call | tf_op jit(solution)/shard_map/pallas_call | solution.py:229
  12.9 0.0 copy-done
  12.9 0.0 copy-done.1
  12.9 0.0 copy-start.3
  12.9 1.9 %shard_map.60 = (bf16[2,4,16,384]{3,2,1,0:T(8,128)(2,1)S(1)}, bf16[2,4,16,384]{3,2,1,0:T(8,128)(2,1)S(1)}, bf16[2,4,16,384]{3,2,1,0:T(8,128)(2,1)S(1)}, bf16[2,4,16,384]{3,2,1,0:T(8,128)(2,1)S(1)}, f32[8,128]{1,0:T(8,128)}) custom-call(bf16[4,16,3072]{2,1,0:T(8,128)(2,1)S(1)} %copy-done, bf16[4,16,3072]{2,1,0:T(8,128)(2,1)S(1)} %copy-done.1, ...), custom_call_target="tpu_custom_call" | custom-call | tf_op jit(solution)/shard_map/pallas_call | solution.py:89
  14.8 0.0 copy-start.2
  14.8 0.7 %collective-permute-start.12 = (bf16[2,4,16,384]{3,2,1,0:T(8,128)(2,1)S(1)}, bf16[2,4,16,384]{3,2,1,0:T(8,128)(2,1)S(1)}, u32[]{:S(2)}, u32[]{:S(2)}) collective-permute-start(bf16[2,4,16,384]{3,2,1,0:T(8,128)(2,1)S(1)} %get-tuple-element.53), channel_id=1, source_target_pairs={{0,4},{4,8},{8,12},{12,0},{1,5},{5,9},{9,13},{13,1},{2,6},{6,10},{... | collective-permute-start | bytes 294920 | tf_op jit(solution)/shard_map/ppermute | solution.py:360
  15.6 0.5 collective-permute-start.13
  16.1 0.0 collective-permute-done.refs_1_.refs_5_
  16.1 2.6 %collective-permute-start.14 = (bf16[2,4,16,384]{3,2,1,0:T(8,128)(2,1)S(1)}, bf16[2,4,16,384]{3,2,1,0:T(8,128)(2,1)S(1)}, u32[]{:S(2)}, u32[]{:S(2)}) collective-permute-start(bf16[2,4,16,384]{3,2,1,0:T(8,128)(2,1)S(1)} %get-tuple-element.55), channel_id=1, source_target_pairs={{0,12},{4,0},{8,4},{12,8},{1,13},{5,1},{9,5},{13,9},{2,14},{6,2},{... | collective-permute-start | bytes 294920 | tf_op jit(solution)/shard_map/ppermute | solution.py:360
  18.7 0.0 collective-permute-done.1.refs_2_.refs_6_
  18.7 0.0 collective-permute-done.2.refs_3_.refs_7_
  18.7 0.0 copy-done.3
  18.7 0.6 %shard_map.57 = (bf16[2,4,2,16,384]{4,3,2,1,0:T(8,128)(2,1)S(1)}, bf16[1,4,2,16,384]{4,3,2,1,0:T(8,128)(2,1)S(1)}, bf16[2,4,2,16,384]{4,3,2,1,0:T(8,128)(2,1)S(1)}) custom-call(s32[8]{0:T(128)S(1)} %get-tuple-element.36.picks_ref, bf16[2,4,16,384]{3,2,1,0:T(8,128)(2,1)S(1)} %copy-done.3, bf16[2,4,16,384]{3,2,1,0:T(8,128)(2,1)S(1)} %collective-permute-done.refs_1_.refs_5_, ...), custom_call_target="tpu_custom_call" | custom-call | tf_op jit(solution)/shard_map/pallas_call | solution.py:131
  19.3 0.0 copy-done.2
  19.3 1.3 %shard_map.58 = (bf16[1,4,16,768]{3,2,1,0:T(8,128)(2,1)S(1)}, bf16[1,4,16,768]{3,2,1,0:T(8,128)(2,1)S(1)}, bf16[1,4,16,768]{3,2,1,0:T(8,128)(2,1)S(1)}, bf16[1,4,16,768]{3,2,1,0:T(8,128)(2,1)S(1)}, f32[8,128]{1,0:T(8,128)}) custom-call(bf16[4,16,3072]{2,1,0:T(8,128)(2,1)S(1)} %copy-done.2, bf16[2,4,2,16,384]{4,3,2,1,0:T(8,128)(2,1)S(1)} %get-tuple-element.41.refs_1_.refs_4_), custom_call_target="tpu_custom_call" | custom-call | tf_op jit(solution)/shard_map/pallas_call | solution.py:89
  20.7 0.6 %collective-permute-start.3 = (bf16[1,4,16,768]{3,2,1,0:T(8,128)(2,1)S(1)}, bf16[1,4,16,768]{3,2,1,0:T(8,128)(2,1)S(1)}, u32[]{:S(2)}, u32[]{:S(2)}) collective-permute-start(bf16[1,4,16,768]{3,2,1,0:T(8,128)(2,1)S(1)} %get-tuple-element.43), channel_id=1, source_target_pairs={{0,4},{4,8},{8,12},{12,0},{1,5},{5,9},{9,13},{13,1},{2,6},{6,10},{... | collective-permute-start | bytes 294920 | tf_op jit(solution)/shard_map/ppermute | solution.py:360
  21.3 0.0 collective-permute-start.6
  21.3 1.2 %collective-permute-done.12.refs_1_.refs_5_ = bf16[2,4,16,384]{3,2,1,0:T(8,128)(2,1)S(1)} collective-permute-done((bf16[2,4,16,384]{3,2,1,0:T(8,128)(2,1)S(1)}, bf16[2,4,16,384]{3,2,1,0:T(8,128)(2,1)S(1)}, u32[]{:S(2)}, u32[]{:S(2)}) %collective-permute-start.12) | collective-permute-done | bytes 98336 | tf_op jit(solution)/shard_map/ppermute | solution.py:360
  22.5 2.8 %collective-permute-start.4 = (bf16[1,4,16,768]{3,2,1,0:T(8,128)(2,1)S(1)}, bf16[1,4,16,768]{3,2,1,0:T(8,128)(2,1)S(1)}, u32[]{:S(2)}, u32[]{:S(2)}) collective-permute-start(bf16[1,4,16,768]{3,2,1,0:T(8,128)(2,1)S(1)} %get-tuple-element.44), channel_id=1, source_target_pairs={{0,8},{4,12},{8,0},{12,4},{1,9},{5,13},{9,1},{13,5},{2,10},{6,14},... | collective-permute-start | bytes 294920 | tf_op jit(solution)/shard_map/ppermute | solution.py:360
  25.3 0.5 collective-permute-done.13.refs_2_.refs_6_
  25.8 2.5 %collective-permute-start.5 = (bf16[1,4,16,768]{3,2,1,0:T(8,128)(2,1)S(1)}, bf16[1,4,16,768]{3,2,1,0:T(8,128)(2,1)S(1)}, u32[]{:S(2)}, u32[]{:S(2)}) collective-permute-start(bf16[1,4,16,768]{3,2,1,0:T(8,128)(2,1)S(1)} %get-tuple-element.45), channel_id=1, source_target_pairs={{0,12},{4,0},{8,4},{12,8},{1,13},{5,1},{9,5},{13,9},{2,14},{6,2},{... | collective-permute-start | bytes 294920 | tf_op jit(solution)/shard_map/ppermute | solution.py:360
  28.3 0.0 collective-permute-done.14.refs_3_.refs_7_
  28.3 2.5 %collective-permute-start.7 = (bf16[1,4,2,16,384]{4,3,2,1,0:T(8,128)(2,1)S(1)}, bf16[1,4,2,16,384]{4,3,2,1,0:T(8,128)(2,1)S(1)}, u32[]{:S(2)}, u32[]{:S(2)}) collective-permute-start(bf16[1,4,2,16,384]{4,3,2,1,0:T(8,128)(2,1)S(1)} %get-tuple-element.46), channel_id=1, source_target_pairs={{0,2},{1,3},{2,0},{3,1},{4,6},{5,7},{6,4},{7,5},{8,10},{9,11},{10,... | collective-permute-start | bytes 294920 | tf_op jit(solution)/shard_map/ppermute | solution.py:360
  30.9 0.0 collective-permute-done.3.refs_1_
  30.9 0.0 collective-permute-start.8
  30.9 0.6 %shard_map.61 = (bf16[2,4,2,16,384]{4,3,2,1,0:T(8,128)(2,1)S(1)}, bf16[1,4,2,16,384]{4,3,2,1,0:T(8,128)(2,1)S(1)}, bf16[2,4,2,16,384]{4,3,2,1,0:T(8,128)(2,1)S(1)}) custom-call(s32[8]{0:T(128)S(1)} %get-tuple-element.36.picks_ref, bf16[2,4,16,384]{3,2,1,0:T(8,128)(2,1)S(1)} %get-tuple-element.52.refs_0_.refs_4_, ...), custom_call_target="tpu_custom_call" | custom-call | flops 99999997952 | tf_op jit(solution)/shard_map/pallas_call | solution.py:131
  31.5 1.7 %collective-permute-done.4.refs_2_ = bf16[1,4,16,768]{3,2,1,0:T(8,128)(2,1)S(1)} collective-permute-done((bf16[1,4,16,768]{3,2,1,0:T(8,128)(2,1)S(1)}, bf16[1,4,16,768]{3,2,1,0:T(8,128)(2,1)S(1)}, u32[]{:S(2)}, u32[]{:S(2)}) %collective-permute-start.4) | collective-permute-done | bytes 98336 | tf_op jit(solution)/shard_map/ppermute | solution.py:360
  33.2 0.0 collective-permute-start.15
  33.2 0.0 collective-permute-done.5.refs_3_
  33.2 1.5 %collective-permute-start.16 = (bf16[1,4,2,16,384]{4,3,2,1,0:T(8,128)(2,1)S(1)}, bf16[1,4,2,16,384]{4,3,2,1,0:T(8,128)(2,1)S(1)}, u32[]{:S(2)}, u32[]{:S(2)}) collective-permute-start(bf16[1,4,2,16,384]{4,3,2,1,0:T(8,128)(2,1)S(1)} %get-tuple-element.57), channel_id=1, source_target_pairs={{0,2},{1,3},{2,0},{3,1},{4,6},{5,7},{6,4},{7,5},{8,10},{9,11},{10,... | collective-permute-start | bytes 294920 | tf_op jit(solution)/shard_map/ppermute | solution.py:360
  34.7 0.0 collective-permute-done.7.refs_9_
  34.7 1.4 %collective-permute-start.17 = (bf16[2,4,2,16,384]{4,3,2,1,0:T(8,128)(2,1)S(1)}, bf16[2,4,2,16,384]{4,3,2,1,0:T(8,128)(2,1)S(1)}, u32[]{:S(2)}, u32[]{:S(2)}) collective-permute-start(bf16[2,4,2,16,384]{4,3,2,1,0:T(8,128)(2,1)S(1)} %get-tuple-element.58), channel_id=1, source_target_pairs={{0,3},{1,0},{2,1},{3,2},{4,7},{5,4},{6,5},{7,6},{8,11},{9,8},{10,9... | collective-permute-start | bytes 589832 | tf_op jit(solution)/shard_map/ppermute | solution.py:360
  36.1 0.0 collective-permute-done.6.refs_8_
  36.1 0.0 collective-permute-done.8.refs_10_
  36.1 2.4 %shard_map.59 = (bf16[4,16,384]{2,1,0:T(8,128)(2,1)S(1)}, bf16[4,16,384]{2,1,0:T(8,128)(2,1)S(1)}, bf16[4,16,384]{2,1,0:T(8,128)(2,1)S(1)}, bf16[4,16,384]{2,1,0:T(8,128)(2,1)S(1)}) custom-call(s32[16]{0:T(128)S(1)} %copy-done.6, f32[4,576]{1,0:T(4,128)S(1)} %get-tuple-element.35.bias_ref.refs_2_, bf16[1,4,16,768]{3,2,1,0:T(8,128)(2,1)S(1)} %get-tuple-element.42.refs_0_, ...), custom_call_target="tpu_custom_call" | custom-call | flops 99999997952 | tf_op jit(solution)/shard_map/pallas_call | solution.py:310
  38.6 1.7 %collective-permute-start.9 = (bf16[4,16,384]{2,1,0:T(8,128)(2,1)S(1)}, bf16[4,16,384]{2,1,0:T(8,128)(2,1)S(1)}, u32[]{:S(2)}, u32[]{:S(2)}) collective-permute-start(bf16[4,16,384]{2,1,0:T(8,128)(2,1)S(1)} %get-tuple-element.49), channel_id=1, source_target_pairs={{0,12},{4,0},{8,4},{12,8},{1,13},{5,1},{9,5},{13,9},{2,14},{6,2},{... | collective-permute-start | bytes 147464 | tf_op jit(solution)/shard_map/ppermute | solution.py:360
  40.3 3.7 %collective-permute-start.10 = (bf16[4,16,384]{2,1,0:T(8,128)(2,1)S(1)}, bf16[4,16,384]{2,1,0:T(8,128)(2,1)S(1)}, u32[]{:S(2)}, u32[]{:S(2)}) collective-permute-start(bf16[4,16,384]{2,1,0:T(8,128)(2,1)S(1)} %get-tuple-element.50), channel_id=1, source_target_pairs={{0,8},{4,12},{8,0},{12,4},{1,9},{5,13},{9,1},{13,5},{2,10},{6,14},... | collective-permute-start | bytes 147464 | tf_op jit(solution)/shard_map/ppermute | solution.py:360
  43.9 0.0 collective-permute-done.16.refs_9_
  43.9 0.0 collective-permute-start.11
  43.9 0.0 collective-permute-done.15.refs_8_
  43.9 0.0 collective-permute-done.17.refs_10_
  43.9 2.5 %shard_map.62 = (bf16[4,16,384]{2,1,0:T(8,128)(2,1)S(1)}, bf16[4,16,384]{2,1,0:T(8,128)(2,1)S(1)}, bf16[4,16,384]{2,1,0:T(8,128)(2,1)S(1)}, bf16[4,16,384]{2,1,0:T(8,128)(2,1)S(1)}) custom-call(s32[16]{0:T(128)S(1)} %copy-done.6, f32[4,576]{1,0:T(4,128)S(1)} %get-tuple-element.35.bias_ref.refs_2_, bf16[1,4,16,768]{3,2,1,0:T(8,128)(2,1)S(1)} %get-tuple-element.42.refs_0_, ...), custom_call_target="tpu_custom_call" | custom-call | tf_op jit(solution)/shard_map/pallas_call | solution.py:310
  46.4 3.9 %collective-permute-start.18 = (bf16[4,16,384]{2,1,0:T(8,128)(2,1)S(1)}, bf16[4,16,384]{2,1,0:T(8,128)(2,1)S(1)}, u32[]{:S(2)}, u32[]{:S(2)}) collective-permute-start(bf16[4,16,384]{2,1,0:T(8,128)(2,1)S(1)} %get-tuple-element.60), channel_id=1, source_target_pairs={{0,12},{4,0},{8,4},{12,8},{1,13},{5,1},{9,5},{13,9},{2,14},{6,2},{... | collective-permute-start | bytes 147464 | tf_op jit(solution)/shard_map/ppermute | solution.py:360
  50.3 0.0 collective-permute-start.19
  50.3 0.0 collective-permute-done.9.refs_1_
  50.3 0.6 %collective-permute-start.20 = (bf16[4,16,384]{2,1,0:T(8,128)(2,1)S(1)}, bf16[4,16,384]{2,1,0:T(8,128)(2,1)S(1)}, u32[]{:S(2)}, u32[]{:S(2)}) collective-permute-start(bf16[4,16,384]{2,1,0:T(8,128)(2,1)S(1)} %get-tuple-element.62), channel_id=1, source_target_pairs={{0,4},{4,8},{8,12},{12,0},{1,5},{5,9},{9,13},{13,1},{2,6},{6,10},{... | collective-permute-start | bytes 147464 | tf_op jit(solution)/shard_map/ppermute | solution.py:360
  50.9 0.0 collective-permute-done.10.refs_2_
  50.9 0.0 collective-permute-done.11.refs_3_
  50.9 1.1 %collective-permute-done.18.refs_5_ = bf16[4,16,384]{2,1,0:T(8,128)(2,1)S(1)} collective-permute-done((bf16[4,16,384]{2,1,0:T(8,128)(2,1)S(1)}, bf16[4,16,384]{2,1,0:T(8,128)(2,1)S(1)}, u32[]{:S(2)}, u32[]{:S(2)}) %collective-permute-start.18) | collective-permute-done | bytes 49184 | tf_op jit(solution)/shard_map/ppermute | solution.py:360
  52.0 3.2 %collective-permute-done.19.refs_6_ = bf16[4,16,384]{2,1,0:T(8,128)(2,1)S(1)} collective-permute-done((bf16[4,16,384]{2,1,0:T(8,128)(2,1)S(1)}, bf16[4,16,384]{2,1,0:T(8,128)(2,1)S(1)}, u32[]{:S(2)}, u32[]{:S(2)}) %collective-permute-start.19) | collective-permute-done | bytes 49184 | tf_op jit(solution)/shard_map/ppermute | solution.py:360
  55.2 0.9 %collective-permute-done.20.refs_7_ = bf16[4,16,384]{2,1,0:T(8,128)(2,1)S(1)} collective-permute-done((bf16[4,16,384]{2,1,0:T(8,128)(2,1)S(1)}, bf16[4,16,384]{2,1,0:T(8,128)(2,1)S(1)}, u32[]{:S(2)}, u32[]{:S(2)}) %collective-permute-start.20) | collective-permute-done | bytes 49184 | tf_op jit(solution)/shard_map/ppermute | solution.py:360
  56.2 0.8 %shard_map.63 = bf16[4,16,3072]{2,1,0:T(8,128)(2,1)} custom-call(bf16[4,16,384]{2,1,0:T(8,128)(2,1)S(1)} %get-tuple-element.48.refs_11_.refs_0_, bf16[4,16,384]{2,1,0:T(8,128)(2,1)S(1)} %collective-permute-done.9.refs_1_, bf16[4,16,384]{2,1,0:T(8,128)(2,1)S(1)} %collective-permute-done.10.refs_2_, bf16[4,16,384]{2,1,0:T(8,128)(2,1)S(1)} %collective-permute-done.11.refs_3_, ...), custom_call_target="tpu_custom_call" | custom-call | tf_op jit(solution)/shard_map/pallas_call | solution.py:348
  (1 shorter events, 0.0 us)
Async XLA Ops:
  0.0 12.9 %copy-start = (bf16[4,16,3072]{2,1,0:T(8,128)(2,1)S(1)}, bf16[4,16,3072]{2,1,0:T(8,128)(2,1)}, u32[]{:S(2)}) copy-start(bf16[4,16,3072]{2,1,0:T(8,128)(2,1)} %refs_0_.5) | copy-start | bytes 1179652
  0.0 12.9 %copy-start.1 = (bf16[4,16,3072]{2,1,0:T(8,128)(2,1)S(1)}, bf16[4,16,3072]{2,1,0:T(8,128)(2,1)}, u32[]{:S(2)}) copy-start(bf16[4,16,3072]{2,1,0:T(8,128)(2,1)} %refs_1_.3) | copy-start | bytes 1179652
  2.9 7.0 %copy-start.4 = (f32[8,128]{1,0:T(8,128)S(1)}, f32[8,128]{1,0:T(8,128)}, u32[]{:S(2)}) copy-start(f32[8,128]{1,0:T(8,128)} %get-tuple-element.34._.refs_3_) | copy-start | bytes 12292
  2.9 13.2 %collective-permute-start = (bf16[2,4,16,384]{3,2,1,0:T(8,128)(2,1)}, bf16[2,4,16,384]{3,2,1,0:T(8,128)(2,1)S(1)}, u32[]{:S(2)}, u32[]{:S(2)}) collective-permute-start(bf16[2,4,16,384]{3,2,1,0:T(8,128)(2,1)} %get-tuple-element.38), channel_id=1, source_target_pairs={{0,4},{4,8},{8,12},{12,0},{1,5},{5,9},{9,13},{13,1},{2,6},{6,10},{... | collective-permute-start | bytes 294920 | tf_op jit(solution)/shard_map/ppermute | solution.py:360
  6.0 12.8 %collective-permute-start.1 = (bf16[2,4,16,384]{3,2,1,0:T(8,128)(2,1)}, bf16[2,4,16,384]{3,2,1,0:T(8,128)(2,1)S(1)}, u32[]{:S(2)}, u32[]{:S(2)}) collective-permute-start(bf16[2,4,16,384]{3,2,1,0:T(8,128)(2,1)} %get-tuple-element.39), channel_id=1, source_target_pairs={{0,8},{4,12},{8,0},{12,4},{1,9},{5,13},{9,1},{13,5},{2,10},{6,14},... | collective-permute-start | bytes 294920 | tf_op jit(solution)/shard_map/ppermute | solution.py:360
  8.5 1.4 %copy-start.6 = (s32[16]{0:T(128)S(1)}, s32[16]{0:T(128)}, u32[]{:S(2)}) copy-start(s32[16]{0:T(128)} %tokens_ref.5) | copy-start | bytes 196
  8.6 10.2 %collective-permute-start.2 = (bf16[2,4,16,384]{3,2,1,0:T(8,128)(2,1)}, bf16[2,4,16,384]{3,2,1,0:T(8,128)(2,1)S(1)}, u32[]{:S(2)}, u32[]{:S(2)}) collective-permute-start(bf16[2,4,16,384]{3,2,1,0:T(8,128)(2,1)} %get-tuple-element.40), channel_id=1, source_target_pairs={{0,12},{4,0},{8,4},{12,8},{1,13},{5,1},{9,5},{13,9},{2,14},{6,2},{... | collective-permute-start | bytes 294920 | tf_op jit(solution)/shard_map/ppermute | solution.py:360
  9.9 0.7 %copy-start.5 = (s32[16,32]{1,0:T(8,128)S(1)}, s32[16,32]{1,0:T(8,128)}, u32[]{:S(2)}) copy-start(s32[16,32]{1,0:T(8,128)} %pair_ref.1) | copy-start | bytes 6148
  12.9 5.8 %copy-start.3 = (bf16[2,4,16,384]{3,2,1,0:T(8,128)(2,1)S(1)}, bf16[2,4,16,384]{3,2,1,0:T(8,128)(2,1)}, u32[]{:S(2)}) copy-start(bf16[2,4,16,384]{3,2,1,0:T(8,128)(2,1)} %get-tuple-element.37.refs_0_.refs_4_) | copy-start | bytes 294916
  14.8 4.5 %copy-start.2 = (bf16[4,16,3072]{2,1,0:T(8,128)(2,1)S(1)}, bf16[4,16,3072]{2,1,0:T(8,128)(2,1)}, u32[]{:S(2)}) copy-start(bf16[4,16,3072]{2,1,0:T(8,128)(2,1)} %refs_0_.4) | copy-start | bytes 1179652
  14.8 7.7 %collective-permute-start.12 = (bf16[2,4,16,384]{3,2,1,0:T(8,128)(2,1)S(1)}, bf16[2,4,16,384]{3,2,1,0:T(8,128)(2,1)S(1)}, u32[]{:S(2)}, u32[]{:S(2)}) collective-permute-start(bf16[2,4,16,384]{3,2,1,0:T(8,128)(2,1)S(1)} %get-tuple-element.53), channel_id=1, source_target_pairs={{0,4},{4,8},{8,12},{12,0},{1,5},{5,9},{9,13},{13,1},{2,6},{6,10},{... | collective-permute-start | bytes 294920 | tf_op jit(solution)/shard_map/ppermute | solution.py:360
  15.6 10.2 %collective-permute-start.13 = (bf16[2,4,16,384]{3,2,1,0:T(8,128)(2,1)S(1)}, bf16[2,4,16,384]{3,2,1,0:T(8,128)(2,1)S(1)}, u32[]{:S(2)}, u32[]{:S(2)}) collective-permute-start(bf16[2,4,16,384]{3,2,1,0:T(8,128)(2,1)S(1)} %get-tuple-element.54), channel_id=1, source_target_pairs={{0,8},{4,12},{8,0},{12,4},{1,9},{5,13},{9,1},{13,5},{2,10},{6,14},... | collective-permute-start | bytes 294920 | tf_op jit(solution)/shard_map/ppermute | solution.py:360
  16.1 12.2 %collective-permute-start.14 = (bf16[2,4,16,384]{3,2,1,0:T(8,128)(2,1)S(1)}, bf16[2,4,16,384]{3,2,1,0:T(8,128)(2,1)S(1)}, u32[]{:S(2)}, u32[]{:S(2)}) collective-permute-start(bf16[2,4,16,384]{3,2,1,0:T(8,128)(2,1)S(1)} %get-tuple-element.55), channel_id=1, source_target_pairs={{0,12},{4,0},{8,4},{12,8},{1,13},{5,1},{9,5},{13,9},{2,14},{6,2},{... | collective-permute-start | bytes 294920 | tf_op jit(solution)/shard_map/ppermute | solution.py:360
  20.7 10.2 %collective-permute-start.3 = (bf16[1,4,16,768]{3,2,1,0:T(8,128)(2,1)S(1)}, bf16[1,4,16,768]{3,2,1,0:T(8,128)(2,1)S(1)}, u32[]{:S(2)}, u32[]{:S(2)}) collective-permute-start(bf16[1,4,16,768]{3,2,1,0:T(8,128)(2,1)S(1)} %get-tuple-element.43), channel_id=1, source_target_pairs={{0,4},{4,8},{8,12},{12,0},{1,5},{5,9},{9,13},{13,1},{2,6},{6,10},{... | collective-permute-start | bytes 294920 | tf_op jit(solution)/shard_map/ppermute | solution.py:360
  21.3 14.8 %collective-permute-start.6 = (bf16[2,4,2,16,384]{4,3,2,1,0:T(8,128)(2,1)S(1)}, bf16[2,4,2,16,384]{4,3,2,1,0:T(8,128)(2,1)S(1)}, u32[]{:S(2)}, u32[]{:S(2)}) collective-permute-start(bf16[2,4,2,16,384]{4,3,2,1,0:T(8,128)(2,1)S(1)} %get-tuple-element.41.refs_1_.refs_4_), channel_id=1, source_target_pairs={{0,1},{1,2},{2,3},{3,0},{4,5},{5,6},{6,7},{7,4},{8,9},{9,10},{10,1... | collective-permute-start | bytes 589832 | tf_op jit(solution)/shard_map/ppermute | solution.py:360
  22.5 10.7 %collective-permute-start.4 = (bf16[1,4,16,768]{3,2,1,0:T(8,128)(2,1)S(1)}, bf16[1,4,16,768]{3,2,1,0:T(8,128)(2,1)S(1)}, u32[]{:S(2)}, u32[]{:S(2)}) collective-permute-start(bf16[1,4,16,768]{3,2,1,0:T(8,128)(2,1)S(1)} %get-tuple-element.44), channel_id=1, source_target_pairs={{0,8},{4,12},{8,0},{12,4},{1,9},{5,13},{9,1},{13,5},{2,10},{6,14},... | collective-permute-start | bytes 294920 | tf_op jit(solution)/shard_map/ppermute | solution.py:360
  25.8 7.4 %collective-permute-start.5 = (bf16[1,4,16,768]{3,2,1,0:T(8,128)(2,1)S(1)}, bf16[1,4,16,768]{3,2,1,0:T(8,128)(2,1)S(1)}, u32[]{:S(2)}, u32[]{:S(2)}) collective-permute-start(bf16[1,4,16,768]{3,2,1,0:T(8,128)(2,1)S(1)} %get-tuple-element.45), channel_id=1, source_target_pairs={{0,12},{4,0},{8,4},{12,8},{1,13},{5,1},{9,5},{13,9},{2,14},{6,2},{... | collective-permute-start | bytes 294920 | tf_op jit(solution)/shard_map/ppermute | solution.py:360
  28.3 6.4 %collective-permute-start.7 = (bf16[1,4,2,16,384]{4,3,2,1,0:T(8,128)(2,1)S(1)}, bf16[1,4,2,16,384]{4,3,2,1,0:T(8,128)(2,1)S(1)}, u32[]{:S(2)}, u32[]{:S(2)}) collective-permute-start(bf16[1,4,2,16,384]{4,3,2,1,0:T(8,128)(2,1)S(1)} %get-tuple-element.46), channel_id=1, source_target_pairs={{0,2},{1,3},{2,0},{3,1},{4,6},{5,7},{6,4},{7,5},{8,10},{9,11},{10,... | collective-permute-start | bytes 294920 | tf_op jit(solution)/shard_map/ppermute | solution.py:360
  30.9 5.3 %collective-permute-start.8 = (bf16[2,4,2,16,384]{4,3,2,1,0:T(8,128)(2,1)S(1)}, bf16[2,4,2,16,384]{4,3,2,1,0:T(8,128)(2,1)S(1)}, u32[]{:S(2)}, u32[]{:S(2)}) collective-permute-start(bf16[2,4,2,16,384]{4,3,2,1,0:T(8,128)(2,1)S(1)} %get-tuple-element.47), channel_id=1, source_target_pairs={{0,3},{1,0},{2,1},{3,2},{4,7},{5,4},{6,5},{7,6},{8,11},{9,8},{10,9... | collective-permute-start | bytes 589832 | tf_op jit(solution)/shard_map/ppermute | solution.py:360
  33.2 10.7 %collective-permute-start.15 = (bf16[2,4,2,16,384]{4,3,2,1,0:T(8,128)(2,1)S(1)}, bf16[2,4,2,16,384]{4,3,2,1,0:T(8,128)(2,1)S(1)}, u32[]{:S(2)}, u32[]{:S(2)}) collective-permute-start(bf16[2,4,2,16,384]{4,3,2,1,0:T(8,128)(2,1)S(1)} %get-tuple-element.56), channel_id=1, source_target_pairs={{0,1},{1,2},{2,3},{3,0},{4,5},{5,6},{6,7},{7,4},{8,9},{9,10},{10,1... | collective-permute-start | bytes 589832 | tf_op jit(solution)/shard_map/ppermute | solution.py:360
  33.2 10.7 %collective-permute-start.16 = (bf16[1,4,2,16,384]{4,3,2,1,0:T(8,128)(2,1)S(1)}, bf16[1,4,2,16,384]{4,3,2,1,0:T(8,128)(2,1)S(1)}, u32[]{:S(2)}, u32[]{:S(2)}) collective-permute-start(bf16[1,4,2,16,384]{4,3,2,1,0:T(8,128)(2,1)S(1)} %get-tuple-element.57), channel_id=1, source_target_pairs={{0,2},{1,3},{2,0},{3,1},{4,6},{5,7},{6,4},{7,5},{8,10},{9,11},{10,... | collective-permute-start | bytes 294920 | tf_op jit(solution)/shard_map/ppermute | solution.py:360
  34.7 9.2 %collective-permute-start.17 = (bf16[2,4,2,16,384]{4,3,2,1,0:T(8,128)(2,1)S(1)}, bf16[2,4,2,16,384]{4,3,2,1,0:T(8,128)(2,1)S(1)}, u32[]{:S(2)}, u32[]{:S(2)}) collective-permute-start(bf16[2,4,2,16,384]{4,3,2,1,0:T(8,128)(2,1)S(1)} %get-tuple-element.58), channel_id=1, source_target_pairs={{0,3},{1,0},{2,1},{3,2},{4,7},{5,4},{6,5},{7,6},{8,11},{9,8},{10,9... | collective-permute-start | bytes 589832 | tf_op jit(solution)/shard_map/ppermute | solution.py:360
  38.6 11.7 %collective-permute-start.9 = (bf16[4,16,384]{2,1,0:T(8,128)(2,1)S(1)}, bf16[4,16,384]{2,1,0:T(8,128)(2,1)S(1)}, u32[]{:S(2)}, u32[]{:S(2)}) collective-permute-start(bf16[4,16,384]{2,1,0:T(8,128)(2,1)S(1)} %get-tuple-element.49), channel_id=1, source_target_pairs={{0,12},{4,0},{8,4},{12,8},{1,13},{5,1},{9,5},{13,9},{2,14},{6,2},{... | collective-permute-start | bytes 147464 | tf_op jit(solution)/shard_map/ppermute | solution.py:360
  40.3 10.6 %collective-permute-start.10 = (bf16[4,16,384]{2,1,0:T(8,128)(2,1)S(1)}, bf16[4,16,384]{2,1,0:T(8,128)(2,1)S(1)}, u32[]{:S(2)}, u32[]{:S(2)}) collective-permute-start(bf16[4,16,384]{2,1,0:T(8,128)(2,1)S(1)} %get-tuple-element.50), channel_id=1, source_target_pairs={{0,8},{4,12},{8,0},{12,4},{1,9},{5,13},{9,1},{13,5},{2,10},{6,14},... | collective-permute-start | bytes 147464 | tf_op jit(solution)/shard_map/ppermute | solution.py:360
  43.9 7.0 %collective-permute-start.11 = (bf16[4,16,384]{2,1,0:T(8,128)(2,1)S(1)}, bf16[4,16,384]{2,1,0:T(8,128)(2,1)S(1)}, u32[]{:S(2)}, u32[]{:S(2)}) collective-permute-start(bf16[4,16,384]{2,1,0:T(8,128)(2,1)S(1)} %get-tuple-element.51), channel_id=1, source_target_pairs={{0,4},{4,8},{8,12},{12,0},{1,5},{5,9},{9,13},{13,1},{2,6},{6,10},{... | collective-permute-start | bytes 147464 | tf_op jit(solution)/shard_map/ppermute | solution.py:360
  46.4 5.6 %collective-permute-start.18 = (bf16[4,16,384]{2,1,0:T(8,128)(2,1)S(1)}, bf16[4,16,384]{2,1,0:T(8,128)(2,1)S(1)}, u32[]{:S(2)}, u32[]{:S(2)}) collective-permute-start(bf16[4,16,384]{2,1,0:T(8,128)(2,1)S(1)} %get-tuple-element.60), channel_id=1, source_target_pairs={{0,12},{4,0},{8,4},{12,8},{1,13},{5,1},{9,5},{13,9},{2,14},{6,2},{... | collective-permute-start | bytes 147464 | tf_op jit(solution)/shard_map/ppermute | solution.py:360
  50.3 5.0 %collective-permute-start.19 = (bf16[4,16,384]{2,1,0:T(8,128)(2,1)S(1)}, bf16[4,16,384]{2,1,0:T(8,128)(2,1)S(1)}, u32[]{:S(2)}, u32[]{:S(2)}) collective-permute-start(bf16[4,16,384]{2,1,0:T(8,128)(2,1)S(1)} %get-tuple-element.61), channel_id=1, source_target_pairs={{0,8},{4,12},{8,0},{12,4},{1,9},{5,13},{9,1},{13,5},{2,10},{6,14},... | collective-permute-start | bytes 147464 | tf_op jit(solution)/shard_map/ppermute | solution.py:360
  50.3 5.9 %collective-permute-start.20 = (bf16[4,16,384]{2,1,0:T(8,128)(2,1)S(1)}, bf16[4,16,384]{2,1,0:T(8,128)(2,1)S(1)}, u32[]{:S(2)}, u32[]{:S(2)}) collective-permute-start(bf16[4,16,384]{2,1,0:T(8,128)(2,1)S(1)} %get-tuple-element.62), channel_id=1, source_target_pairs={{0,4},{4,8},{8,12},{12,0},{1,5},{5,9},{9,13},{13,1},{2,6},{6,10},{... | collective-permute-start | bytes 147464 | tf_op jit(solution)/shard_map/ppermute | solution.py:360
where the time goes:
time: 57.2 us; the launch traced here: 57 us
  starting transfers between devices  32.2 us (56%)
  Pallas kernels  15.2 us (27%)
  waiting for transfers between devices  8.68 us (15%)
  local copies, waits for them, and re-layouts  0.73 us (1%)
    ppermute x21, starting transfers between devices, shifted(): lax.ppermute(array, axis, [(i, (i + distance) % count) for i in range(cou...  32.2 us
    ppermute x21, waiting for transfers between devices, shifted(): lax.ppermute(array, axis, [(i, (i + distance) % count) for i in range(cou...  8.68 us
    pallas_call x3, Pallas kernels, rotate_pieces(): pl.pallas_call(functools.partial(rotate_kernel, (tuple(range(count)), sta...  6.09 us
    pallas_call x2, Pallas kernels, attend(): pl.pallas_call(functools.partial(attend_kernel, counts, start), in_specs=...  4.89 us
    pallas_call x1, Pallas kernels, plan(): pl.pallas_call(functools.partial(plan_kernel, count_head, count_tm, block...  2.25 us
    pallas_call x2, Pallas kernels, pick_blocks(): pl.pallas_call(functools.partial(pick_kernel, count_head, count_tm, len(o...  1.2 us
  transfers between devices with their start and end apart: 21, of which 6 were waited for; matrix products, arithmetic and copies ran while one was open for 0% of the time, Pallas kernels for 20%

commit v1 on v0

--- a/solution.py
+++ b/solution.py
@@ -41,66 +41,67 @@
     return block.astype(jnp.float32).reshape(rows, width).astype(block.dtype)
 
 
-def by_distance(refs, count, direction, axis="head"):
-    if len(refs) > 1:
-        return list(refs)
-    me = lax.axis_index(axis)
-    return [refs[0].at[lax.rem(me + direction * s + count, count)] for s in range(count)]
-
-
-def rotate_kernel(group, count_head, skipped, *refs):
-    ids, start, size = group
-    count = len(ids)
-    sources, outs = refs[:count], by_distance(refs[count + skipped : -3], count_head, 1)
-    token, buffer, sems = refs[-3:]
+def fields_of(message):
+    at, fields = 0, []
+    for source, start, size in message:
+        fields.append((source, start, size, at))
+        at += size
+    return fields, at
+
+
+def rotate_kernel(message, sources, count_head, skipped, *refs):
+    fields, total = fields_of(message)
+    ins = dict(zip(sources, refs))
+    outs, (token, buffer, sems) = refs[len(sources) + skipped : -3], refs[-3:]
     token[...] = jnp.zeros_like(token)
-    blocks, tokens, width = sources[0].shape
+    blocks, tokens, width = refs[0].shape
     width_here = width // count_head
     me = lax.axis_index("head")
     order = list(range(1, count_head)) + [0]
     copies = {}
     for s in order:
         goal = lax.rem(me + s, count_head)
-        column = pl.multiple_of(goal * width_here + start, HD)
-        for k, source in enumerate(sources):
-            copies[s, k] = pltpu.make_async_copy(
-                source.at[:, :, pl.ds(column, size)], buffer.at[s, k], sems.at[s, k]
+        for f, (source, start, size, at) in enumerate(fields):
+            column = pl.multiple_of(goal * width_here + start, HD)
+            copies[s, f] = pltpu.make_async_copy(
+                ins[source].at[:, :, pl.ds(column, size)],
+                buffer.at[s, :, :, pl.ds(at, size)],
+                sems.at[s, f],
             )
-            copies[s, k].start()
+            copies[s, f].start()
     sign = sign_matrix()
     for s in order:
-        for k in range(count):
-            copies[s, k].wait()
-            flat = rows_of(buffer[s, k])
+        for f, (_, _, size, start) in enumerate(fields):
+            copies[s, f].wait()
+            flat = rows_of(buffer[s, :, :, start : start + size])
             heads = [flat[:, at : at + HD] for at in range(0, size, HD)]
             turned = jnp.dot(
                 jnp.concatenate(heads, axis=0), sign, preferred_element_type=jnp.float32
             )
             turned = (turned * ROTATE_SCALE).reshape(size // HD, blocks, tokens, HD)
             for h in range(size // HD):
-                outs[s][k, :, :, h * HD : (h + 1) * HD] = turned[h].astype(jnp.bfloat16)
-
-
-def rotate_pieces(sources, start, size, count_head, stacked, after=(), limit=VMEM):
-    blocks, tokens, _ = sources[0].shape
-    count = len(sources)
-    one = (count, blocks, tokens, size)
-    shapes = [(count_head,) + one] if stacked else [one] * count_head
+                at = start + h * HD
+                outs[s][:, :, at : at + HD] = turned[h].astype(jnp.bfloat16)
+
+
+def rotate_pieces(arrays, message, count_head, after=(), limit=VMEM):
+    blocks, tokens, _ = arrays[0].shape
+    fields, total = fields_of(message)
+    sources = sorted({source for source, _, _ in message})
+    one = (blocks, tokens, total)
     *pieces, token = pl.pallas_call(
-        functools.partial(
-            rotate_kernel, (tuple(range(count)), start, size), count_head, len(after)
-        ),
-        in_specs=[pl.BlockSpec(memory_space=pltpu.HBM)] * count
+        functools.partial(rotate_kernel, message, sources, count_head, len(after)),
+        in_specs=[pl.BlockSpec(memory_space=pltpu.HBM)] * len(sources)
         + [pl.BlockSpec(memory_space=pl.ANY)] * len(after),
-        out_specs=[pl.BlockSpec(memory_space=pltpu.VMEM)] * (len(shapes) + 1),
-        out_shape=[jax.ShapeDtypeStruct(shape, jnp.bfloat16) for shape in shapes] + [TOKEN],
+        out_specs=[pl.BlockSpec(memory_space=pltpu.VMEM)] * (count_head + 1),
+        out_shape=[jax.ShapeDtypeStruct(one, jnp.bfloat16)] * count_head + [TOKEN],
         scratch_shapes=[
             pltpu.VMEM((count_head,) + one, jnp.bfloat16),
-            pltpu.SemaphoreType.DMA((count_head, count)),
+            pltpu.SemaphoreType.DMA((count_head, len(fields))),
         ],
         cost_estimate=NO_COST,
         compiler_params=pltpu.CompilerParams(vmem_limit_bytes=limit),
-    )(*sources, *after)
+    )(*[arrays[source] for source in sources], *after)
     return pieces, token
 
 
@@ -108,36 +109,34 @@
     return NEAR_CAP if distance in (1, count_tm - 1) else FAR_CAP
 
 
-def pick_kernel(count_head, count_tm, own_count, skipped, picks_ref, *refs):
-    pieces = by_distance(refs[:own_count], count_head, -1)
-    outs = by_distance(refs[own_count + skipped :], count_tm, 1, "tm")[-(count_tm - 1) :]
+def pick_kernel(count_head, count_tm, lanes, skipped, picks_ref, *refs):
+    pieces, outs = refs[:count_head], refs[count_head + skipped :]
     shard = lax.axis_index("tm")
     for distance, out in enumerate(outs, 1):
         goal = lax.rem(shard + distance, count_tm)
         for k in range(slots_at(distance, count_tm)):
             pick = picks_ref[NEAR_CAP * goal + k]
             for s in range(count_head):
-                out[k, s] = pieces[s][:, pick]
-
-
-def pick_blocks(picks, owns, count_head, count_tm, stacked, after=(), cost=NO_COST):
-    kinds, _, tokens, width = owns[0].shape[-4:]
-    one = (count_head, kinds, tokens, width)
-    if stacked:
-        shapes = [(count_tm, NEAR_CAP) + one]
-    else:
-        shapes = [(slots_at(distance, count_tm),) + one for distance in range(1, count_tm)]
+                out[k, s] = pieces[s][pick, :, lanes[0] : lanes[1]]
+
+
+def pick_blocks(picks, pieces, lanes, count_tm, after, cost):
+    count_head = len(pieces)
+    one = (count_head, pieces[0].shape[1], lanes[1] - lanes[0])
     vmem = pl.BlockSpec(memory_space=pltpu.VMEM)
     return pl.pallas_call(
-        functools.partial(pick_kernel, count_head, count_tm, len(owns), len(after)),
+        functools.partial(pick_kernel, count_head, count_tm, lanes, len(after)),
         in_specs=[pl.BlockSpec(memory_space=pltpu.SMEM)]
-        + [vmem] * len(owns)
+        + [vmem] * count_head
         + [pl.BlockSpec(memory_space=pl.ANY)] * len(after),
-        out_specs=[vmem] * len(shapes),
-        out_shape=[jax.ShapeDtypeStruct(shape, jnp.bfloat16) for shape in shapes],
+        out_specs=[vmem] * (count_tm - 1),
+        out_shape=[
+            jax.ShapeDtypeStruct((slots_at(distance, count_tm),) + one, jnp.bfloat16)
+            for distance in range(1, count_tm)
+        ],
         cost_estimate=cost,
         compiler_params=pltpu.CompilerParams(vmem_limit_bytes=VMEM),
-    )(picks, *owns, *after)
+    )(picks, *pieces, *after)
 
 
 def remote_rows(count_tm):
@@ -248,29 +247,30 @@
     )(pair_list, block_tokens, after)
 
 
-def attend_kernel(counts, start, tokens_ref, bias_ref, *refs):
-    count_head, count_tm, query_count, own_count, slot_count, skipped = counts
-    at = [query_count, query_count + own_count, query_count + own_count + slot_count]
-    queries = by_distance(refs[: at[0]], count_head, -1)
-    owns = by_distance(refs[at[0] : at[1]], count_head, -1)
-    slots = by_distance(refs[at[1] : at[2]], count_tm, -1, "tm")[-(count_tm - 1) :]
-    outs = by_distance(refs[at[2] + skipped :], count_head, -1)
-    _, blocks, tokens, size = owns[0].shape
+def attend_kernel(counts, at, size, tokens_ref, bias_ref, *refs):
+    count_head, count_tm, skipped = counts
+    query_at, key_at = at
+    queries, owns = refs[:count_head], refs[count_head : 2 * count_head]
+    slots = refs[2 * count_head : 2 * count_head + count_tm - 1]
+    outs = refs[2 * count_head + count_tm - 1 + skipped :]
+    blocks, tokens, _ = owns[0].shape
     shard = lax.axis_index("tm")
     me = lax.axis_index("head")
     sign = sign_matrix()
     for h in range(size // HD):
         lanes = slice(h * HD, (h + 1) * HD)
-        query_lanes = slice(start + h * HD, start + (h + 1) * HD)
+        query_lanes = slice(query_at + h * HD, query_at + (h + 1) * HD)
         query = jnp.concatenate(
-            [rows_of(queries[s][0, i, :, query_lanes]) for i in range(blocks) for s in range(count_head)],
+            [rows_of(queries[s][i, :, query_lanes]) for i in range(blocks) for s in range(count_head)],
             axis=0,
         )
 
         def gathered(kind):
-            pieces = [rows_of(own[kind, :, :, lanes]) for own in owns]
+            first = kind * size + h * HD
+            own_lanes = slice(key_at + first, key_at + first + HD)
+            pieces = [rows_of(own[:, :, own_lanes]) for own in owns]
             pieces += [
-                rows_of(slots[distance - 1][k, :, kind, :, lanes])
+                rows_of(slots[distance - 1][k, :, :, first : first + HD])
                 for distance, k in remote_rows(count_tm)
             ]
             return jnp.concatenate(pieces, axis=0)
@@ -302,55 +302,53 @@
                 ).astype(jnp.bfloat16)
 
 
-def attend(block_tokens, bias, start, queries, owns, slots, count_head, count_tm, after, cost):
-    _, blocks, tokens, size = owns[0].shape[-4:]
-    shapes = [(blocks, tokens, size)] * count_head
-    counts = (count_head, count_tm, len(queries), len(owns), len(slots), len(after))
+def attend(block_tokens, bias, queries, query_at, owns, key_at, slots, size, after, cost):
+    count_head, count_tm = len(owns), len(slots) + 1
+    blocks, tokens, _ = owns[0].shape
     vmem = pl.BlockSpec(memory_space=pltpu.VMEM)
     return pl.pallas_call(
-        functools.partial(attend_kernel, counts, start),
+        functools.partial(
+            attend_kernel, (count_head, count_tm, len(after)), (query_at, key_at), size
+        ),
         in_specs=[pl.BlockSpec(memory_space=pltpu.SMEM)]
-        + [vmem] * (1 + len(queries) + len(owns) + len(slots))
+        + [vmem] * (2 * count_head + count_tm)
         + [pl.BlockSpec(memory_space=pl.ANY)] * len(after),
-        out_specs=[vmem] * len(shapes),
-        out_shape=[jax.ShapeDtypeStruct(shape, jnp.bfloat16) for shape in shapes],
+        out_specs=[vmem] * count_head,
+        out_shape=[jax.ShapeDtypeStruct((blocks, tokens, size), jnp.bfloat16)] * count_head,
         cost_estimate=cost,
         compiler_params=pltpu.CompilerParams(vmem_limit_bytes=VMEM),
     )(block_tokens, bias, *queries, *owns, *slots, *after)
 
 
-def place_kernel(counts, starts, width_here, *refs):
-    count_head = counts[0]
-    out_ref, sems = refs[-2:]
+def place_kernel(count_head, starts, width_here, *refs):
+    pieces, out_ref, sems = refs[:-2], refs[-2], refs[-1]
+    me = lax.axis_index("head")
     copies = []
-    at = 0
-    for count, start in zip(counts[1:], starts):
-        pieces = by_distance(refs[at : at + count], count_head, 1)
-        at += count
-        for s, piece in enumerate(pieces):
-            column = lax.rem(lax.axis_index("head") + s, count_head) * width_here + start
-            copies.append(
-                pltpu.make_async_copy(
-                    piece,
-                    out_ref.at[:, :, pl.ds(pl.multiple_of(column, HD), piece.shape[-1])],
-                    sems.at[len(copies)],
-                )
+    for at, piece in enumerate(pieces):
+        part, s = at // count_head, at % count_head
+        column = lax.rem(me + s, count_head) * width_here + starts[part]
+        copies.append(
+            pltpu.make_async_copy(
+                piece,
+                out_ref.at[:, :, pl.ds(pl.multiple_of(column, HD), piece.shape[-1])],
+                sems.at[at],
             )
-            copies[-1].start()
+        )
+        copies[-1].start()
     for copy in copies:
         copy.wait()
 
 
-def place_pieces(parts, starts, count_head, width_here):
+def place_pieces(parts, starts, width_here):
+    count_head = len(parts[0])
     pieces = [piece for part in parts for piece in part]
-    blocks, tokens, _ = pieces[0].shape[-3:]
-    counts = (count_head,) + tuple(len(part) for part in parts)
+    blocks, tokens, _ = pieces[0].shape
     return pl.pallas_call(
-        functools.partial(place_kernel, counts, starts, width_here),
+        functools.partial(place_kernel, count_head, starts, width_here),
         in_specs=[pl.BlockSpec(memory_space=pl.ANY)] * len(pieces),
         out_specs=pl.BlockSpec(memory_space=pltpu.HBM),
         out_shape=jax.ShapeDtypeStruct((blocks, tokens, count_head * width_here), jnp.bfloat16),
-        scratch_shapes=[pltpu.SemaphoreType.DMA((len(parts) * count_head,))],
+        scratch_shapes=[pltpu.SemaphoreType.DMA((len(pieces),))],
         compiler_params=pltpu.CompilerParams(vmem_limit_bytes=VMEM),
     )(*pieces)
 
@@ -361,16 +359,12 @@
 
 
 def exchange(pieces, direction):
-    if len(pieces) == 1:
-        return [lax.all_to_all(pieces[0], "head", split_axis=0, concat_axis=0, tiled=True)]
     return [pieces[0]] + [
         shifted(piece, "head", direction * s) for s, piece in enumerate(pieces[1:], 1)
     ]
 
 
 def forward(sent):
-    if len(sent) == 1:
-        return [lax.all_to_all(sent[0], "tm", split_axis=0, concat_axis=0, tiled=True)]
     return [shifted(block, "tm", distance) for distance, block in enumerate(sent, 1)]
 
 
@@ -380,35 +374,45 @@
     blocks, tokens, width = query_rows.shape
     width_here = width // count_head
     heads = width_here // HD
-    cut = (heads + 1) // 2 * HD
+    cut = (2 * heads + 2) // 3 * HD
     parts = [(0, cut), (cut, width_here - cut)] if heads > 1 else [(0, width_here)]
-    sources = [key_rows, value_rows]
-    pieces, token = rotate_pieces(sources, *parts[0], count_head, False, limit=WIDE_VMEM)
+    arrays = [query_rows, key_rows, value_rows]
+    messages = []
+    for at, part in enumerate(parts):
+        message = [(1,) + part, (2,) + part]
+        messages.append(message + ([(0,) + parts[at - 1]] if at else []))
+    messages.append([(0,) + parts[-1]])
+    key_at = [0] * len(parts)
+    query_at = [2 * size for _, size in parts[1:]] + [0]
+
+    pieces, token = rotate_pieces(arrays, messages[0], count_head, limit=WIDE_VMEM)
     packed = [pieces]
     picks, bias = plan(pair_list, block_tokens, token, blocks, count_head, count_tm)
-    for part in parts[1:]:
-        pieces, token = rotate_pieces(sources, *part, count_head, False, after=(bias, token))
+    after = (bias,)
+    for message in messages[1:-1]:
+        pieces, token = rotate_pieces(arrays, message, count_head, after)
         packed.append(pieces)
-    key_values = [exchange(pieces, 1) for pieces in packed]
-    sent = [pick_blocks(picks, key_values[0], count_head, count_tm, False)]
-    for owns in key_values[1:]:
-        sent.append(
-            pick_blocks(
-                picks, owns, count_head, count_tm, False, after=(sent[-1][0],), cost=HIGH_COST
-            )
-        )
-    query, _ = rotate_pieces([query_rows], 0, width_here, count_head, False, after=(sent[0][0],))
-    queries = exchange(query, 1)
+        after = (token,)
+    received = [exchange(pieces, 1) for pieces in packed]
+    sent, after = [], ()
+    for at, (_, size) in enumerate(parts):
+        lanes = (key_at[at], key_at[at] + 2 * size)
+        cost = HIGH_COST if at else NO_COST
+        sent.append(pick_blocks(picks, received[at], lanes, count_tm, after, cost))
+        after = (sent[-1][0],)
+        if not at:
+            pieces, _ = rotate_pieces(arrays, messages[-1], count_head, after)
+    received.append(exchange(pieces, 1))
     returned, after = [], ()
-    for at, (owns, picked) in enumerate(zip(key_values, sent)):
+    for at, (_, size) in enumerate(parts):
         cost = NO_COST if at == len(parts) - 1 else HIGH_COST
-        slots, start = forward(picked), parts[at][0]
         attended = attend(
-            block_tokens, bias, start, queries, owns, slots, count_head, count_tm, after, cost
+            block_tokens, bias, received[at + 1], query_at[at], received[at], key_at[at],
+            forward(sent[at]), size, after, cost,
         )
         after = (attended[0],)
         returned.append(exchange(attended, -1))
-    return place_pieces(returned, [start for start, _ in parts], count_head, width_here)
+    return place_pieces(returned, [start for start, _ in parts], width_here)
 
 
 def solution(mesh):

time: 57.2 us -> 58.9 us (1.030)
  starting transfers between devices: 32.2 us -> 30.7 us
  waiting for transfers between devices: 8.68 us -> 9.77 us
  Pallas kernels: 15.2 us -> 16.2 us
  local copies, waits for them, and re-layouts: 0.73 us -> 1.71 us
    ppermute x21, starting transfers between devices: 32.2 us -> 30.7 us  [shifted(): lax.ppermute(array, axis, [(i, (i + distance) % count) for i in range(cou...]
    ppermute x21, waiting for transfers between devices: 8.68 us -> 9.77 us  [shifted(): lax.ppermute(array, axis, [(i, (i + distance) % count) for i in range(cou...]
    unnamed x14 -> x16, local copies, waits for them, and re-layouts: 0.73 us -> 1.71 us
    pallas_call x8, Pallas kernels: 13 us -> 13.9 us  [the longest x3 6.71 us: rotate_pieces(): pl.pallas_call(functools.partial(rotate_kernel, message, sources, count_h...]
  transfers between devices with their start and end apart: 21 -> 21, of which waited for: 6 -> 5; matrix products, arithmetic and copies ran while one was open for 0% -> 0% of each run, Pallas kernels for 20% -> 17%
where the time goes in v1:
time: 58.9 us; the launch traced here: 58.6 us
  starting transfers between devices  30.7 us (52%)
  Pallas kernels  16.2 us (28%)
  waiting for transfers between devices  9.77 us (17%)
  local copies, waits for them, and re-layouts  1.71 us (3%)
    ppermute x21, starting transfers between devices, shifted(): lax.ppermute(array, axis, [(i, (i + distance) % count) for i in range(cou...  30.7 us
    ppermute x21, waiting for transfers between devices, shifted(): lax.ppermute(array, axis, [(i, (i + distance) % count) for i in range(cou...  9.77 us
    pallas_call x3, Pallas kernels, rotate_pieces(): pl.pallas_call(functools.partial(rotate_kernel, message, sources, count_h...  6.71 us
    pallas_call x2, Pallas kernels, attend(): pl.pallas_call(functools.partial(attend_kernel, (count_head, count_tm, le...  5.23 us
    pallas_call x1, Pallas kernels, plan(): pl.pallas_call(functools.partial(plan_kernel, count_head, count_tm, block...  2.25 us
    unnamed x16, local copies, waits for them, and re-layouts  1.71 us
  transfers between devices with their start and end apart: 21, of which 5 were waited for; matrix products, arithmetic and copies ran while one was open for 0% of the time, Pallas kernels for 17%

profile of v1, /device:TPU:0, one launch (start us, length us, event | category | flops | bytes accessed | tf_op | source)
XLA Modules:
  0.0 58.6 jit_solution(4857724688235154386)
XLA Ops:
  0.0 0.0 copy-start
  0.0 0.0 copy-start.1
  0.0 3.0 %shard_map.55 = (bf16[4,16,1024]{2,1,0:T(8,128)(2,1)}, bf16[4,16,1024]{2,1,0:T(8,128)(2,1)}, bf16[4,16,1024]{2,1,0:T(8,128)(2,1)}, bf16[4,16,1024]{2,1,0:T(8,128)(2,1)}, f32[8,128]{1,0:T(8,128)}) custom-call(bf16[4,16,3072]{2,1,0:T(8,128)(2,1)} %refs_1_.3, bf16[4,16,3072]{2,1,0:T(8,128)(2,1)} %refs_2_.1), custom_call_target="tpu_custom_call" | custom-call | tf_op jit(solution)/shard_map/pallas_call | solution.py:92
  3.0 0.0 copy-start.6
  3.0 3.1 %collective-permute-start.3 = (bf16[4,16,1024]{2,1,0:T(8,128)(2,1)}, bf16[4,16,1024]{2,1,0:T(8,128)(2,1)S(1)}, u32[]{:S(2)}, u32[]{:S(2)}) collective-permute-start(bf16[4,16,1024]{2,1,0:T(8,128)(2,1)} %get-tuple-element.41), channel_id=1, source_target_pairs={{0,4},{4,8},{8,12},{12,0},{1,5},{5,9},{9,13},{13,1},{2,6},{6,10},{... | collective-permute-start | bytes 393224 | tf_op jit(solution)/shard_map/ppermute | solution.py:358
  6.1 2.6 %collective-permute-start.4 = (bf16[4,16,1024]{2,1,0:T(8,128)(2,1)}, bf16[4,16,1024]{2,1,0:T(8,128)(2,1)S(1)}, u32[]{:S(2)}, u32[]{:S(2)}) collective-permute-start(bf16[4,16,1024]{2,1,0:T(8,128)(2,1)} %get-tuple-element.42), channel_id=1, source_target_pairs={{0,8},{4,12},{8,0},{12,4},{1,9},{5,13},{9,1},{13,5},{2,10},{6,14},... | collective-permute-start | bytes 393224 | tf_op jit(solution)/shard_map/ppermute | solution.py:358
  8.7 1.3 %collective-permute-start.5 = (bf16[4,16,1024]{2,1,0:T(8,128)(2,1)}, bf16[4,16,1024]{2,1,0:T(8,128)(2,1)S(1)}, u32[]{:S(2)}, u32[]{:S(2)}) collective-permute-start(bf16[4,16,1024]{2,1,0:T(8,128)(2,1)} %get-tuple-element.43), channel_id=1, source_target_pairs={{0,12},{4,0},{8,4},{12,8},{1,13},{5,1},{9,5},{13,9},{2,14},{6,2},{... | collective-permute-start | bytes 393224 | tf_op jit(solution)/shard_map/ppermute | solution.py:358
  10.0 0.0 copy-done.6
  10.0 0.0 copy-done.7
  10.0 0.7 %copy-done.5 = s32[16,32]{1,0:T(8,128)S(1)} copy-done((s32[16,32]{1,0:T(8,128)S(1)}, s32[16,32]{1,0:T(8,128)}, u32[]{:S(2)}) %copy-start.5) | copy-done | bytes 2072
  10.7 2.3 %shard_map.56 = (s32[8]{0:T(128)S(1)}, f32[4,576]{1,0:T(4,128)S(1)}) custom-call(s32[16,32]{1,0:T(8,128)S(1)} %copy-done.5, s32[16]{0:T(128)S(1)} %copy-done.7, f32[8,128]{1,0:T(8,128)S(1)} %copy-done.6), custom_call_target="tpu_custom_call" | custom-call | tf_op jit(solution)/shard_map/pallas_call | solution.py:228
  13.0 0.0 copy-done
  13.0 0.0 copy-done.1
  13.0 0.0 copy-start.2
  13.0 1.0 %copy-done.2 = bf16[4,16,3072]{2,1,0:T(8,128)(2,1)S(1)} copy-done((bf16[4,16,3072]{2,1,0:T(8,128)(2,1)S(1)}, bf16[4,16,3072]{2,1,0:T(8,128)(2,1)}, u32[]{:S(2)}) %copy-start.2) | copy-done | bytes 393240
  14.0 2.5 %shard_map.57 = (bf16[4,16,1024]{2,1,0:T(8,128)(2,1)S(1)}, bf16[4,16,1024]{2,1,0:T(8,128)(2,1)S(1)}, bf16[4,16,1024]{2,1,0:T(8,128)(2,1)S(1)}, bf16[4,16,1024]{2,1,0:T(8,128)(2,1)S(1)}, f32[8,128]{1,0:T(8,128)}) custom-call(bf16[4,16,3072]{2,1,0:T(8,128)(2,1)S(1)} %copy-done.2, bf16[4,16,3072]{2,1,0:T(8,128)(2,1)S(1)} %copy-done, ...), custom_call_target="tpu_custom_call" | custom-call | tf_op jit(solution)/shard_map/pallas_call | solution.py:92
  16.5 0.0 copy-start.3
  16.6 0.7 %collective-permute-start = (bf16[4,16,1024]{2,1,0:T(8,128)(2,1)S(1)}, bf16[4,16,1024]{2,1,0:T(8,128)(2,1)S(1)}, u32[]{:S(2)}, u32[]{:S(2)}) collective-permute-start(bf16[4,16,1024]{2,1,0:T(8,128)(2,1)S(1)} %get-tuple-element.37), channel_id=1, source_target_pairs={{0,4},{4,8},{8,12},{12,0},{1,5},{5,9},{9,13},{13,1},{2,6},{6,10},{... | collective-permute-start | bytes 393224 | tf_op jit(solution)/shard_map/ppermute | solution.py:358
  17.3 0.5 collective-permute-start.1
  17.8 0.0 collective-permute-done.3.refs_1_.refs_5_
  17.8 2.6 %collective-permute-start.2 = (bf16[4,16,1024]{2,1,0:T(8,128)(2,1)S(1)}, bf16[4,16,1024]{2,1,0:T(8,128)(2,1)S(1)}, u32[]{:S(2)}, u32[]{:S(2)}) collective-permute-start(bf16[4,16,1024]{2,1,0:T(8,128)(2,1)S(1)} %get-tuple-element.39), channel_id=1, source_target_pairs={{0,12},{4,0},{8,4},{12,8},{1,13},{5,1},{9,5},{13,9},{2,14},{6,2},{... | collective-permute-start | bytes 393224 | tf_op jit(solution)/shard_map/ppermute | solution.py:358
  20.4 0.0 collective-permute-done.4.refs_2_.refs_6_
  20.4 0.0 collective-permute-done.5.refs_3_.refs_7_
  20.4 0.0 copy-done.4
  20.5 0.6 %shard_map.58 = (bf16[2,4,16,1024]{3,2,1,0:T(8,128)(2,1)S(1)}, bf16[1,4,16,1024]{3,2,1,0:T(8,128)(2,1)S(1)}, bf16[2,4,16,1024]{3,2,1,0:T(8,128)(2,1)S(1)}) custom-call(s32[8]{0:T(128)S(1)} %get-tuple-element.44.picks_ref, bf16[4,16,1024]{2,1,0:T(8,128)(2,1)S(1)} %copy-done.4, bf16[4,16,1024]{2,1,0:T(8,128)(2,1)S(1)} %collective-permute-done.3.refs_1_.refs_5_, ...), custom_call_target="tpu_custom_call" | custom-call | tf_op jit(solution)/shard_map/pallas_call | solution.py:127
  21.1 0.1 collective-permute-start.6
  21.1 0.0 copy-done.3
  21.1 1.2 %shard_map.60 = (bf16[4,16,256]{2,1,0:T(8,128)(2,1)S(1)}, bf16[4,16,256]{2,1,0:T(8,128)(2,1)S(1)}, bf16[4,16,256]{2,1,0:T(8,128)(2,1)}, bf16[4,16,256]{2,1,0:T(8,128)(2,1)S(1)}, f32[8,128]{1,0:T(8,128)}) custom-call(bf16[4,16,3072]{2,1,0:T(8,128)(2,1)S(1)} %copy-done.3, bf16[2,4,16,1024]{3,2,1,0:T(8,128)(2,1)S(1)} %get-tuple-element.45.refs_1_.refs_4_), custom_call_target="tpu_custom_call" | custom-call | tf_op jit(solution)/shard_map/pallas_call | solution.py:92
  22.3 1.6 %collective-permute-start.7 = (bf16[1,4,16,1024]{3,2,1,0:T(8,128)(2,1)S(1)}, bf16[1,4,16,1024]{3,2,1,0:T(8,128)(2,1)S(1)}, u32[]{:S(2)}, u32[]{:S(2)}) collective-permute-start(bf16[1,4,16,1024]{3,2,1,0:T(8,128)(2,1)S(1)} %get-tuple-element.46), channel_id=1, source_target_pairs={{0,2},{1,3},{2,0},{3,1},{4,6},{5,7},{6,4},{7,5},{8,10},{9,11},{10,... | collective-permute-start | bytes 393224 | tf_op jit(solution)/shard_map/ppermute | solution.py:358
  23.9 1.0 %collective-permute-done.refs_1_.refs_5_ = bf16[4,16,1024]{2,1,0:T(8,128)(2,1)S(1)} collective-permute-done((bf16[4,16,1024]{2,1,0:T(8,128)(2,1)S(1)}, bf16[4,16,1024]{2,1,0:T(8,128)(2,1)S(1)}, u32[]{:S(2)}, u32[]{:S(2)}) %collective-permute-start) | collective-permute-done | bytes 131104 | tf_op jit(solution)/shard_map/ppermute | solution.py:358
  24.9 0.4 collective-permute-start.8
  25.3 3.4 %collective-permute-done.1.refs_2_.refs_6_ = bf16[4,16,1024]{2,1,0:T(8,128)(2,1)S(1)} collective-permute-done((bf16[4,16,1024]{2,1,0:T(8,128)(2,1)S(1)}, bf16[4,16,1024]{2,1,0:T(8,128)(2,1)S(1)}, u32[]{:S(2)}, u32[]{:S(2)}) %collective-permute-start.1) | collective-permute-done | bytes 131104 | tf_op jit(solution)/shard_map/ppermute | solution.py:358
  28.8 1.5 %collective-permute-start.12 = (bf16[4,16,256]{2,1,0:T(8,128)(2,1)S(1)}, bf16[4,16,256]{2,1,0:T(8,128)(2,1)S(1)}, u32[]{:S(2)}, u32[]{:S(2)}) collective-permute-start(bf16[4,16,256]{2,1,0:T(8,128)(2,1)S(1)} %get-tuple-element.53), channel_id=1, source_target_pairs={{0,4},{4,8},{8,12},{12,0},{1,5},{5,9},{9,13},{13,1},{2,6},{6,10},{... | collective-permute-start | bytes 98312 | tf_op jit(solution)/shard_map/ppermute | solution.py:358
  30.3 0.0 collective-permute-done.2.refs_3_.refs_7_
  30.3 3.4 %collective-permute-start.13 = (bf16[4,16,256]{2,1,0:T(8,128)(2,1)}, bf16[4,16,256]{2,1,0:T(8,128)(2,1)}, u32[]{:S(2)}, u32[]{:S(2)}) collective-permute-start(bf16[4,16,256]{2,1,0:T(8,128)(2,1)} %get-tuple-element.54), channel_id=1, source_target_pairs={{0,8},{4,12},{8,0},{12,4},{1,9},{5,13},{9,1},{13,5},{2,10},{6,14},... | collective-permute-start | bytes 98312 | tf_op jit(solution)/shard_map/ppermute | solution.py:358
  33.7 0.6 shard_map.61
  34.3 0.7 %collective-permute-done.12.refs_1_ = bf16[4,16,256]{2,1,0:T(8,128)(2,1)S(1)} collective-permute-done((bf16[4,16,256]{2,1,0:T(8,128)(2,1)S(1)}, bf16[4,16,256]{2,1,0:T(8,128)(2,1)S(1)}, u32[]{:S(2)}, u32[]{:S(2)}) %collective-permute-start.12) | collective-permute-done | bytes 32800 | tf_op jit(solution)/shard_map/ppermute | solution.py:358
  35.0 2.0 %collective-permute-start.14 = (bf16[4,16,256]{2,1,0:T(8,128)(2,1)S(1)}, bf16[4,16,256]{2,1,0:T(8,128)(2,1)S(1)}, u32[]{:S(2)}, u32[]{:S(2)}) collective-permute-start(bf16[4,16,256]{2,1,0:T(8,128)(2,1)S(1)} %get-tuple-element.55), channel_id=1, source_target_pairs={{0,12},{4,0},{8,4},{12,8},{1,13},{5,1},{9,5},{13,9},{2,14},{6,2},{... | collective-permute-start | bytes 98312 | tf_op jit(solution)/shard_map/ppermute | solution.py:358
  37.0 0.0 collective-permute-done.7.refs_9_
  37.0 0.0 collective-permute-start.15
  37.0 0.0 collective-permute-done.6.refs_8_
  37.0 1.6 %collective-permute-start.16 = (bf16[1,4,16,512]{3,2,1,0:T(8,128)(2,1)S(1)}, bf16[1,4,16,512]{3,2,1,0:T(8,128)(2,1)S(1)}, u32[]{:S(2)}, u32[]{:S(2)}) collective-permute-start(bf16[1,4,16,512]{3,2,1,0:T(8,128)(2,1)S(1)} %get-tuple-element.57), channel_id=1, source_target_pairs={{0,2},{1,3},{2,0},{3,1},{4,6},{5,7},{6,4},{7,5},{8,10},{9,11},{10,... | collective-permute-start | bytes 196616 | tf_op jit(solution)/shard_map/ppermute | solution.py:358
  38.6 0.0 collective-permute-done.8.refs_10_
  38.6 1.4 %collective-permute-start.17 = (bf16[2,4,16,512]{3,2,1,0:T(8,128)(2,1)S(1)}, bf16[2,4,16,512]{3,2,1,0:T(8,128)(2,1)S(1)}, u32[]{:S(2)}, u32[]{:S(2)}) collective-permute-start(bf16[2,4,16,512]{3,2,1,0:T(8,128)(2,1)S(1)} %get-tuple-element.58), channel_id=1, source_target_pairs={{0,3},{1,0},{2,1},{3,2},{4,7},{5,4},{6,5},{7,6},{8,11},{9,8},{10,9... | collective-permute-start | bytes 393224 | tf_op jit(solution)/shard_map/ppermute | solution.py:358
  40.0 3.1 %shard_map.59 = (bf16[4,16,512]{2,1,0:T(8,128)(2,1)S(1)}, bf16[4,16,512]{2,1,0:T(8,128)(2,1)S(1)}, bf16[4,16,512]{2,1,0:T(8,128)(2,1)S(1)}, bf16[4,16,512]{2,1,0:T(8,128)(2,1)S(1)}) custom-call(s32[16]{0:T(128)S(1)} %copy-done.7, f32[4,576]{1,0:T(4,128)S(1)} %get-tuple-element.35.refs_3_.bias_ref, ...), custom_call_target="tpu_custom_call" | custom-call | flops 99999997952 | tf_op jit(solution)/shard_map/pallas_call | solution.py:309
  43.1 0.0 collective-permute-done.13.refs_2_
  43.1 0.0 collective-permute-done.14.refs_3_
  43.1 0.0 collective-permute-done.16.refs_9_
  43.1 0.0 collective-permute-done.15.refs_8_
  43.1 0.1 collective-permute-done.17.refs_10_
  43.2 2.2 %shard_map.62 = (bf16[4,16,256]{2,1,0:T(8,128)(2,1)S(1)}, bf16[4,16,256]{2,1,0:T(8,128)(2,1)S(1)}, bf16[4,16,256]{2,1,0:T(8,128)(2,1)S(1)}, bf16[4,16,256]{2,1,0:T(8,128)(2,1)S(1)}) custom-call(s32[16]{0:T(128)S(1)} %copy-done.7, f32[4,576]{1,0:T(4,128)S(1)} %get-tuple-element.35.refs_3_.bias_ref, bf16[4,16,256]{2,1,0:T(8,128)(2,1)S(1)} %get-tuple-element.52.refs_0_, ...), custom_call_target="tpu_custom_call" | custom-call | tf_op jit(solution)/shard_map/pallas_call | solution.py:309
  45.4 0.1 collective-permute-start.18
  45.5 0.2 collective-permute-start.9
  45.7 3.3 %collective-permute-start.10 = (bf16[4,16,512]{2,1,0:T(8,128)(2,1)S(1)}, bf16[4,16,512]{2,1,0:T(8,128)(2,1)S(1)}, u32[]{:S(2)}, u32[]{:S(2)}) collective-permute-start(bf16[4,16,512]{2,1,0:T(8,128)(2,1)S(1)} %get-tuple-element.50), channel_id=1, source_target_pairs={{0,8},{4,12},{8,0},{12,4},{1,9},{5,13},{9,1},{13,5},{2,10},{6,14},... | collective-permute-start | bytes 196616 | tf_op jit(solution)/shard_map/ppermute | solution.py:358
  48.9 0.0 collective-permute-start.11
  48.9 1.5 %collective-permute-start.19 = (bf16[4,16,256]{2,1,0:T(8,128)(2,1)S(1)}, bf16[4,16,256]{2,1,0:T(8,128)(2,1)S(1)}, u32[]{:S(2)}, u32[]{:S(2)}) collective-permute-start(bf16[4,16,256]{2,1,0:T(8,128)(2,1)S(1)} %get-tuple-element.61), channel_id=1, source_target_pairs={{0,8},{4,12},{8,0},{12,4},{1,9},{5,13},{9,1},{13,5},{2,10},{6,14},... | collective-permute-start | bytes 98312 | tf_op jit(solution)/shard_map/ppermute | solution.py:358
  50.5 0.0 collective-permute-done.18.refs_5_
  50.5 2.9 %collective-permute-start.20 = (bf16[4,16,256]{2,1,0:T(8,128)(2,1)S(1)}, bf16[4,16,256]{2,1,0:T(8,128)(2,1)S(1)}, u32[]{:S(2)}, u32[]{:S(2)}) collective-permute-start(bf16[4,16,256]{2,1,0:T(8,128)(2,1)S(1)} %get-tuple-element.62), channel_id=1, source_target_pairs={{0,4},{4,8},{8,12},{12,0},{1,5},{5,9},{9,13},{13,1},{2,6},{6,10},{... | collective-permute-start | bytes 98312 | tf_op jit(solution)/shard_map/ppermute | solution.py:358
  53.3 4.4 %collective-permute-done.19.refs_6_ = bf16[4,16,256]{2,1,0:T(8,128)(2,1)S(1)} collective-permute-done((bf16[4,16,256]{2,1,0:T(8,128)(2,1)S(1)}, bf16[4,16,256]{2,1,0:T(8,128)(2,1)S(1)}, u32[]{:S(2)}, u32[]{:S(2)}) %collective-permute-start.19) | collective-permute-done | bytes 32800 | tf_op jit(solution)/shard_map/ppermute | solution.py:358
  57.8 0.0 collective-permute-done.20.refs_7_
  57.8 0.0 collective-permute-done.9.refs_1_
  57.8 0.0 collective-permute-done.10.refs_2_
  57.8 0.0 collective-permute-done.11.refs_3_
  57.8 0.8 %shard_map.63 = bf16[4,16,3072]{2,1,0:T(8,128)(2,1)} custom-call(bf16[4,16,512]{2,1,0:T(8,128)(2,1)S(1)} %get-tuple-element.48.refs_11_.refs_0_, bf16[4,16,512]{2,1,0:T(8,128)(2,1)S(1)} %collective-permute-done.9.refs_1_, bf16[4,16,512]{2,1,0:T(8,128)(2,1)S(1)} %collective-permute-done.10.refs_2_, bf16[4,16,512]{2,1,0:T(8,128)(2,1)S(1)} %collective-permute-done.11.refs_3_, ...), custom_call_target="tpu_custom_call" | custom-call | tf_op jit(solution)/shard_map/pallas_call | solution.py:346
  (3 shorter events, 0.0 us)
Async XLA Ops:
  0.0 13.0 %copy-start = (bf16[4,16,3072]{2,1,0:T(8,128)(2,1)S(1)}, bf16[4,16,3072]{2,1,0:T(8,128)(2,1)}, u32[]{:S(2)}) copy-start(bf16[4,16,3072]{2,1,0:T(8,128)(2,1)} %refs_1_.3) | copy-start | bytes 1179652
  0.0 13.0 %copy-start.1 = (bf16[4,16,3072]{2,1,0:T(8,128)(2,1)S(1)}, bf16[4,16,3072]{2,1,0:T(8,128)(2,1)}, u32[]{:S(2)}) copy-start(bf16[4,16,3072]{2,1,0:T(8,128)(2,1)} %refs_2_.1) | copy-start | bytes 1179652
  3.0 7.0 %copy-start.6 = (f32[8,128]{1,0:T(8,128)S(1)}, f32[8,128]{1,0:T(8,128)}, u32[]{:S(2)}) copy-start(f32[8,128]{1,0:T(8,128)} %get-tuple-element.34._) | copy-start | bytes 12292
  3.0 14.8 %collective-permute-start.3 = (bf16[4,16,1024]{2,1,0:T(8,128)(2,1)}, bf16[4,16,1024]{2,1,0:T(8,128)(2,1)S(1)}, u32[]{:S(2)}, u32[]{:S(2)}) collective-permute-start(bf16[4,16,1024]{2,1,0:T(8,128)(2,1)} %get-tuple-element.41), channel_id=1, source_target_pairs={{0,4},{4,8},{8,12},{12,0},{1,5},{5,9},{9,13},{13,1},{2,6},{6,10},{... | collective-permute-start | bytes 393224 | tf_op jit(solution)/shard_map/ppermute | solution.py:358
  6.1 14.4 %collective-permute-start.4 = (bf16[4,16,1024]{2,1,0:T(8,128)(2,1)}, bf16[4,16,1024]{2,1,0:T(8,128)(2,1)S(1)}, u32[]{:S(2)}, u32[]{:S(2)}) collective-permute-start(bf16[4,16,1024]{2,1,0:T(8,128)(2,1)} %get-tuple-element.42), channel_id=1, source_target_pairs={{0,8},{4,12},{8,0},{12,4},{1,9},{5,13},{9,1},{13,5},{2,10},{6,14},... | collective-permute-start | bytes 393224 | tf_op jit(solution)/shard_map/ppermute | solution.py:358
  8.7 1.4 %copy-start.7 = (s32[16]{0:T(128)S(1)}, s32[16]{0:T(128)}, u32[]{:S(2)}) copy-start(s32[16]{0:T(128)} %tokens_ref.5) | copy-start | bytes 196
  8.7 11.8 %collective-permute-start.5 = (bf16[4,16,1024]{2,1,0:T(8,128)(2,1)}, bf16[4,16,1024]{2,1,0:T(8,128)(2,1)S(1)}, u32[]{:S(2)}, u32[]{:S(2)}) collective-permute-start(bf16[4,16,1024]{2,1,0:T(8,128)(2,1)} %get-tuple-element.43), channel_id=1, source_target_pairs={{0,12},{4,0},{8,4},{12,8},{1,13},{5,1},{9,5},{13,9},{2,14},{6,2},{... | collective-permute-start | bytes 393224 | tf_op jit(solution)/shard_map/ppermute | solution.py:358
  10.0 0.7 %copy-start.5 = (s32[16,32]{1,0:T(8,128)S(1)}, s32[16,32]{1,0:T(8,128)}, u32[]{:S(2)}) copy-start(s32[16,32]{1,0:T(8,128)} %pair_ref.1) | copy-start | bytes 6148
  13.0 1.0 %copy-start.2 = (bf16[4,16,3072]{2,1,0:T(8,128)(2,1)S(1)}, bf16[4,16,3072]{2,1,0:T(8,128)(2,1)}, u32[]{:S(2)}) copy-start(bf16[4,16,3072]{2,1,0:T(8,128)(2,1)} %refs_0_.5) | copy-start | bytes 1179652
  14.0 6.4 %copy-start.4 = (bf16[4,16,1024]{2,1,0:T(8,128)(2,1)S(1)}, bf16[4,16,1024]{2,1,0:T(8,128)(2,1)}, u32[]{:S(2)}) copy-start(bf16[4,16,1024]{2,1,0:T(8,128)(2,1)} %get-tuple-element.40.refs_0_.refs_4_) | copy-start | bytes 393220
  16.5 4.6 %copy-start.3 = (bf16[4,16,3072]{2,1,0:T(8,128)(2,1)S(1)}, bf16[4,16,3072]{2,1,0:T(8,128)(2,1)}, u32[]{:S(2)}) copy-start(bf16[4,16,3072]{2,1,0:T(8,128)(2,1)} %refs_0_.5) | copy-start | bytes 1179652
  16.6 8.3 %collective-permute-start = (bf16[4,16,1024]{2,1,0:T(8,128)(2,1)S(1)}, bf16[4,16,1024]{2,1,0:T(8,128)(2,1)S(1)}, u32[]{:S(2)}, u32[]{:S(2)}) collective-permute-start(bf16[4,16,1024]{2,1,0:T(8,128)(2,1)S(1)} %get-tuple-element.37), channel_id=1, source_target_pairs={{0,4},{4,8},{8,12},{12,0},{1,5},{5,9},{9,13},{13,1},{2,6},{6,10},{... | collective-permute-start | bytes 393224 | tf_op jit(solution)/shard_map/ppermute | solution.py:358
  17.3 11.5 %collective-permute-start.1 = (bf16[4,16,1024]{2,1,0:T(8,128)(2,1)S(1)}, bf16[4,16,1024]{2,1,0:T(8,128)(2,1)S(1)}, u32[]{:S(2)}, u32[]{:S(2)}) collective-permute-start(bf16[4,16,1024]{2,1,0:T(8,128)(2,1)S(1)} %get-tuple-element.38), channel_id=1, source_target_pairs={{0,8},{4,12},{8,0},{12,4},{1,9},{5,13},{9,1},{13,5},{2,10},{6,14},... | collective-permute-start | bytes 393224 | tf_op jit(solution)/shard_map/ppermute | solution.py:358
  17.8 12.5 %collective-permute-start.2 = (bf16[4,16,1024]{2,1,0:T(8,128)(2,1)S(1)}, bf16[4,16,1024]{2,1,0:T(8,128)(2,1)S(1)}, u32[]{:S(2)}, u32[]{:S(2)}) collective-permute-start(bf16[4,16,1024]{2,1,0:T(8,128)(2,1)S(1)} %get-tuple-element.39), channel_id=1, source_target_pairs={{0,12},{4,0},{8,4},{12,8},{1,13},{5,1},{9,5},{13,9},{2,14},{6,2},{... | collective-permute-start | bytes 393224 | tf_op jit(solution)/shard_map/ppermute | solution.py:358
  21.1 16.0 %collective-permute-start.6 = (bf16[2,4,16,1024]{3,2,1,0:T(8,128)(2,1)S(1)}, bf16[2,4,16,1024]{3,2,1,0:T(8,128)(2,1)S(1)}, u32[]{:S(2)}, u32[]{:S(2)}) collective-permute-start(bf16[2,4,16,1024]{3,2,1,0:T(8,128)(2,1)S(1)} %get-tuple-element.45.refs_1_.refs_4_), channel_id=1, source_target_pairs={{0,1},{1,2},{2,3},{3,0},{4,5},{5,6},{6,7},{7,4},{8,9},{9,10},{10,1... | collective-permute-start | bytes 786440 | tf_op jit(solution)/shard_map/ppermute | solution.py:358
  22.3 14.7 %collective-permute-start.7 = (bf16[1,4,16,1024]{3,2,1,0:T(8,128)(2,1)S(1)}, bf16[1,4,16,1024]{3,2,1,0:T(8,128)(2,1)S(1)}, u32[]{:S(2)}, u32[]{:S(2)}) collective-permute-start(bf16[1,4,16,1024]{3,2,1,0:T(8,128)(2,1)S(1)} %get-tuple-element.46), channel_id=1, source_target_pairs={{0,2},{1,3},{2,0},{3,1},{4,6},{5,7},{6,4},{7,5},{8,10},{9,11},{10,... | collective-permute-start | bytes 393224 | tf_op jit(solution)/shard_map/ppermute | solution.py:358
  24.9 13.7 %collective-permute-start.8 = (bf16[2,4,16,1024]{3,2,1,0:T(8,128)(2,1)S(1)}, bf16[2,4,16,1024]{3,2,1,0:T(8,128)(2,1)S(1)}, u32[]{:S(2)}, u32[]{:S(2)}) collective-permute-start(bf16[2,4,16,1024]{3,2,1,0:T(8,128)(2,1)S(1)} %get-tuple-element.47), channel_id=1, source_target_pairs={{0,3},{1,0},{2,1},{3,2},{4,7},{5,4},{6,5},{7,6},{8,11},{9,8},{10,9... | collective-permute-start | bytes 786440 | tf_op jit(solution)/shard_map/ppermute | solution.py:358
  28.8 6.2 %collective-permute-start.12 = (bf16[4,16,256]{2,1,0:T(8,128)(2,1)S(1)}, bf16[4,16,256]{2,1,0:T(8,128)(2,1)S(1)}, u32[]{:S(2)}, u32[]{:S(2)}) collective-permute-start(bf16[4,16,256]{2,1,0:T(8,128)(2,1)S(1)} %get-tuple-element.53), channel_id=1, source_target_pairs={{0,4},{4,8},{8,12},{12,0},{1,5},{5,9},{9,13},{13,1},{2,6},{6,10},{... | collective-permute-start | bytes 98312 | tf_op jit(solution)/shard_map/ppermute | solution.py:358
  30.3 12.8 %collective-permute-start.13 = (bf16[4,16,256]{2,1,0:T(8,128)(2,1)}, bf16[4,16,256]{2,1,0:T(8,128)(2,1)}, u32[]{:S(2)}, u32[]{:S(2)}) collective-permute-start(bf16[4,16,256]{2,1,0:T(8,128)(2,1)} %get-tuple-element.54), channel_id=1, source_target_pairs={{0,8},{4,12},{8,0},{12,4},{1,9},{5,13},{9,1},{13,5},{2,10},{6,14},... | collective-permute-start | bytes 98312 | tf_op jit(solution)/shard_map/ppermute | solution.py:358
  35.0 8.1 %collective-permute-start.14 = (bf16[4,16,256]{2,1,0:T(8,128)(2,1)S(1)}, bf16[4,16,256]{2,1,0:T(8,128)(2,1)S(1)}, u32[]{:S(2)}, u32[]{:S(2)}) collective-permute-start(bf16[4,16,256]{2,1,0:T(8,128)(2,1)S(1)} %get-tuple-element.55), channel_id=1, source_target_pairs={{0,12},{4,0},{8,4},{12,8},{1,13},{5,1},{9,5},{13,9},{2,14},{6,2},{... | collective-permute-start | bytes 98312 | tf_op jit(solution)/shard_map/ppermute | solution.py:358
  37.0 6.1 %collective-permute-start.15 = (bf16[2,4,16,512]{3,2,1,0:T(8,128)(2,1)S(1)}, bf16[2,4,16,512]{3,2,1,0:T(8,128)(2,1)S(1)}, u32[]{:S(2)}, u32[]{:S(2)}) collective-permute-start(bf16[2,4,16,512]{3,2,1,0:T(8,128)(2,1)S(1)} %get-tuple-element.56), channel_id=1, source_target_pairs={{0,1},{1,2},{2,3},{3,0},{4,5},{5,6},{6,7},{7,4},{8,9},{9,10},{10,1... | collective-permute-start | bytes 393224 | tf_op jit(solution)/shard_map/ppermute | solution.py:358
  37.0 6.1 %collective-permute-start.16 = (bf16[1,4,16,512]{3,2,1,0:T(8,128)(2,1)S(1)}, bf16[1,4,16,512]{3,2,1,0:T(8,128)(2,1)S(1)}, u32[]{:S(2)}, u32[]{:S(2)}) collective-permute-start(bf16[1,4,16,512]{3,2,1,0:T(8,128)(2,1)S(1)} %get-tuple-element.57), channel_id=1, source_target_pairs={{0,2},{1,3},{2,0},{3,1},{4,6},{5,7},{6,4},{7,5},{8,10},{9,11},{10,... | collective-permute-start | bytes 196616 | tf_op jit(solution)/shard_map/ppermute | solution.py:358
  38.6 4.6 %collective-permute-start.17 = (bf16[2,4,16,512]{3,2,1,0:T(8,128)(2,1)S(1)}, bf16[2,4,16,512]{3,2,1,0:T(8,128)(2,1)S(1)}, u32[]{:S(2)}, u32[]{:S(2)}) collective-permute-start(bf16[2,4,16,512]{3,2,1,0:T(8,128)(2,1)S(1)} %get-tuple-element.58), channel_id=1, source_target_pairs={{0,3},{1,0},{2,1},{3,2},{4,7},{5,4},{6,5},{7,6},{8,11},{9,8},{10,9... | collective-permute-start | bytes 393224 | tf_op jit(solution)/shard_map/ppermute | solution.py:358
  45.4 5.1 %collective-permute-start.18 = (bf16[4,16,256]{2,1,0:T(8,128)(2,1)S(1)}, bf16[4,16,256]{2,1,0:T(8,128)(2,1)S(1)}, u32[]{:S(2)}, u32[]{:S(2)}) collective-permute-start(bf16[4,16,256]{2,1,0:T(8,128)(2,1)S(1)} %get-tuple-element.60), channel_id=1, source_target_pairs={{0,12},{4,0},{8,4},{12,8},{1,13},{5,1},{9,5},{13,9},{2,14},{6,2},{... | collective-permute-start | bytes 98312 | tf_op jit(solution)/shard_map/ppermute | solution.py:358
  45.5 12.3 %collective-permute-start.9 = (bf16[4,16,512]{2,1,0:T(8,128)(2,1)S(1)}, bf16[4,16,512]{2,1,0:T(8,128)(2,1)S(1)}, u32[]{:S(2)}, u32[]{:S(2)}) collective-permute-start(bf16[4,16,512]{2,1,0:T(8,128)(2,1)S(1)} %get-tuple-element.49), channel_id=1, source_target_pairs={{0,12},{4,0},{8,4},{12,8},{1,13},{5,1},{9,5},{13,9},{2,14},{6,2},{... | collective-permute-start | bytes 196616 | tf_op jit(solution)/shard_map/ppermute | solution.py:358
  45.7 12.1 %collective-permute-start.10 = (bf16[4,16,512]{2,1,0:T(8,128)(2,1)S(1)}, bf16[4,16,512]{2,1,0:T(8,128)(2,1)S(1)}, u32[]{:S(2)}, u32[]{:S(2)}) collective-permute-start(bf16[4,16,512]{2,1,0:T(8,128)(2,1)S(1)} %get-tuple-element.50), channel_id=1, source_target_pairs={{0,8},{4,12},{8,0},{12,4},{1,9},{5,13},{9,1},{13,5},{2,10},{6,14},... | collective-permute-start | bytes 196616 | tf_op jit(solution)/shard_map/ppermute | solution.py:358
  48.9 8.8 %collective-permute-start.11 = (bf16[4,16,512]{2,1,0:T(8,128)(2,1)S(1)}, bf16[4,16,512]{2,1,0:T(8,128)(2,1)S(1)}, u32[]{:S(2)}, u32[]{:S(2)}) collective-permute-start(bf16[4,16,512]{2,1,0:T(8,128)(2,1)S(1)} %get-tuple-element.51), channel_id=1, source_target_pairs={{0,4},{4,8},{8,12},{12,0},{1,5},{5,9},{9,13},{13,1},{2,6},{6,10},{... | collective-permute-start | bytes 196616 | tf_op jit(solution)/shard_map/ppermute | solution.py:358
  48.9 8.8 %collective-permute-start.19 = (bf16[4,16,256]{2,1,0:T(8,128)(2,1)S(1)}, bf16[4,16,256]{2,1,0:T(8,128)(2,1)S(1)}, u32[]{:S(2)}, u32[]{:S(2)}) collective-permute-start(bf16[4,16,256]{2,1,0:T(8,128)(2,1)S(1)} %get-tuple-element.61), channel_id=1, source_target_pairs={{0,8},{4,12},{8,0},{12,4},{1,9},{5,13},{9,1},{13,5},{2,10},{6,14},... | collective-permute-start | bytes 98312 | tf_op jit(solution)/shard_map/ppermute | solution.py:358
  50.5 7.3 %collective-permute-start.20 = (bf16[4,16,256]{2,1,0:T(8,128)(2,1)S(1)}, bf16[4,16,256]{2,1,0:T(8,128)(2,1)S(1)}, u32[]{:S(2)}, u32[]{:S(2)}) collective-permute-start(bf16[4,16,256]{2,1,0:T(8,128)(2,1)S(1)} %get-tuple-element.62), channel_id=1, source_target_pairs={{0,4},{4,8},{8,12},{12,0},{1,5},{5,9},{9,13},{13,1},{2,6},{6,10},{... | collective-permute-start | bytes 98312 | tf_op jit(solution)/shard_map/ppermute | solution.py:358
